TPU v7x, 32 devices: a whole 2x2x4 slice. The times are simulated.
32 devices in a mesh: row: 8 (over z, y), col: 4 (over x, core).
Axes of the slice: x: 2, y: 2, z: 4, core: 2. Of those that a mesh axis runs over, the one named last changes fastest.
Arguments:
- positions: float32 [3, 4096], P(None, ('row', 'col')), may hold values from 0 to 1
- radii: float32 [4096], P(('row', 'col')), may hold values from 0.5 to 2
- right_side: float32 [4096, 256], P(('row', 'col')), may hold values from -60 to 60, as said below
Outputs:
- solution: float32 [4096, 256], P(('row', 'col'))
- residual: float32 [4096, 256], P(('row', 'col'))
Inputs may be any that keep to these rules, and one draw needn't show every extreme that they name: `right_side`: real values of varying scale.
All inputs are finite; a program needn't handle non-finite values.
Results may differ from a plain program's by a relative error of at most 0.0003.
Values sent between devices are 32-bit elements; how exact they have to be, the bound alone decides.
No kernel may reach another device: no remote copies, remote signals or barrier semaphores. Data moves between devices by JAX's collectives and lax.ppermute only.
A program may use at most 64 MiB of HBM per device.

v0:
```python
import jax
import jax.numpy as jnp
from jax import lax
from jax.sharding import PartitionSpec as P

ITERS = 2


def kernel_product(row_points, col_points, values, kernel_scale, softening, limit):
    row_count = row_points.shape[1]
    col_count = col_points.shape[1]
    blocks = max(1, row_count * col_count // limit)
    while row_count % blocks:
        blocks = blocks - 1
    block_size = row_count // blocks
    grouped = row_points.reshape(3, blocks, block_size).transpose(1, 0, 2)

    def apply_block(row_block):
        first = row_block[0][:, None] - col_points[0][None, :]
        second = row_block[1][:, None] - col_points[1][None, :]
        third = row_block[2][:, None] - col_points[2][None, :]
        squared = first * first + second * second + third * third
        weights = lax.rsqrt(squared + softening) * kernel_scale
        return jnp.dot(
            weights, values, preferred_element_type=jnp.float32, precision=lax.Precision.HIGHEST
        )

    return lax.map(apply_block, grouped).reshape(row_count, values.shape[1])


def constants(total):
    kernel_scale = float(total) ** (-0.5)
    spacing = 0.25 * float(total) ** (-1.0 / 3.0)
    return (kernel_scale, spacing * spacing)


def squares(residual):
    return lax.psum(jnp.sum(residual * residual, axis=0), ("row", "col"))


def body(positions, radii, right_side):
    local_count = positions.shape[1]
    total = local_count * lax.axis_size("row") * lax.axis_size("col")
    kernel_scale, softening = constants(total)
    row_points = lax.all_gather(positions, "col", axis=1, tiled=True)
    col_points = lax.all_gather(positions, "row", axis=1, tiled=True)
    limit = 1 << 20
    solution = jnp.zeros_like(right_side)
    residual = right_side
    direction = right_side
    norm_now = squares(residual)
    for iteration in range(ITERS):
        col_values = lax.all_gather(direction, "row", axis=0, tiled=True)
        summed = lax.psum_scatter(
            kernel_product(row_points, col_points, col_values, kernel_scale, softening, limit),
            "col",
            scatter_dimension=0,
            tiled=True,
        )
        image_vec = direction / radii[:, None] + summed
        curvature = lax.psum(jnp.sum(direction * image_vec, axis=0), ("row", "col"))
        step_size = norm_now / curvature
        solution = solution + step_size * direction
        residual = residual - step_size * image_vec
        if iteration + 1 < ITERS:
            norm_next = squares(residual)
            direction = residual + norm_next / norm_now * direction
            norm_now = norm_next
    return (solution, residual)


def solution(mesh):
    return jax.shard_map(
        body,
        mesh=mesh,
        in_specs=(P(None, ("row", "col")), P(("row", "col")), P(("row", "col"), None)),
        out_specs=(P(("row", "col"), None), P(("row", "col"), None)),
        check_vma=False,
    )
```

profile of v0, /device:TPU:0, one launch (start us, length us, event | category | flops | bytes accessed | tf_op | source)
XLA Modules:
  0.0 275.4 jit_solution(13990938444437012334)
XLA Ops:
  7.2 0.0 all-gather.3.cloned.1.call-start
  7.2 0.7 all-gather.3.cloned.1.call-update
  7.9 0.0 reduce-scatter.3.cloned.1.call-start
  7.9 6.3 %all_gather.12 = f32[3,512]{1,0:T(4,128)S(1)} all-gather(f32[3,128]{1,0:T(4,128)} %param.3), channel_id=1, replica_groups=mesh['row'=8,'col'=4] {'col'}, dimensions={1}, use_global_device_ids=true | all-gather | bytes 7680 | tf_op jit(solution)/shard_map/all_gather | solution.py:45
  14.2 27.0 %all_gather.13 = f32[3,1024]{1,0:T(4,128)S(1)} all-gather(f32[3,128]{1,0:T(4,128)} %param.3), channel_id=1, replica_groups=mesh['row'=8,'col'=4] {'row'}, dimensions={1}, use_global_device_ids=true | all-gather | bytes 13824 | tf_op jit(solution)/shard_map/all_gather | solution.py:46
  41.3 11.8 %all-gather.3.cloned.1.call-done = f32[1024,256]{1,0:T(8,128)} async-done(((f32[128,256]{1,0:T(8,128)}), f32[1024,256]{1,0:T(8,128)}) %all-gather.3.cloned.1.call-update) | async-done | bytes 1048592 | tf_op jit(solution)/shard_map/all_gather | solution.py:53
  53.1 0.0 copy-start
  53.1 0.0 copy-start.2
  53.1 4.6 %fusion.1 = f32[512,256]{1,0:T(8,128)} fusion(f32[1024,256]{1,0:T(8,128)} %all-gather.3.cloned.1.call-done, f32[1024]{0:T(1024)S(1)} %bitcast.10, f32[512]{0:T(512)S(1)} %bitcast.16, f32[1024]{0:T(1024)S(1)} %bitcast.12, f32[512]{0:T(512)S(1)} %bitcast.18, f32[1024]{0:T(1024)S(1)} %bitcast.8, f32[512]{0:T(512)S(1)} %bitcast.14), kind=kOutput, calls=%fused_computation.2 | convolution fusion | flops 1615855616 | bytes 1591296 | tf_op jit(solution)/shard_map/while/body/eval_jaxpr/dot_general | solution.py:24
  57.7 0.0 reduce-scatter.3.cloned.1.call-update
  57.7 0.0 all-gather.5.cloned.1.call-start
  57.8 20.5 %reduce-scatter.3.cloned.1.call-done = f32[128,256]{1,0:T(8,128)} async-done(((f32[512,256]{1,0:T(8,128)}), f32[128,256]{1,0:T(8,128)}) %reduce-scatter.3.cloned.1.call-update) | async-done | bytes 131088 | tf_op jit(solution)/shard_map/reduce_scatter | solution.py:54
  78.3 0.0 copy-done
  78.3 0.0 copy-done.2
  78.3 1.0 multiply_reduce_fusion.2
  79.3 39.4 %all-reduce = (f32[256]{0:T(256)S(1)}, f32[256]{0:T(256)S(1)}) all-reduce(f32[256]{0:T(256)S(1)} %get-tuple-element.23, f32[256]{0:T(256)S(1)} %get-tuple-element.22), channel_id=1, replica_groups=mesh['row'=8,'col'=4] {'row','col'}, use_global_device_ids=true, to_apply=%region_1.0 | all-reduce | flops 512 | bytes 4096 | tf_op jit(solution)/shard_map/psum | solution.py:38
  118.7 1.0 multiply_reduce_fusion.1
  119.7 41.0 %psum.30 = f32[256]{0:T(256)S(1)} all-reduce(f32[256]{0:T(256)S(1)} %get-tuple-element.31), channel_id=1, replica_groups=mesh['row'=8,'col'=4] {'row','col'}, use_global_device_ids=true, to_apply=%region_6.7 | all-reduce | flops 256 | bytes 2048 | tf_op jit(solution)/shard_map/psum | solution.py:38
  160.7 0.7 multiply_add_fusion.1
  161.4 0.0 all-gather.5.cloned.1.call-update
  161.4 0.0 copy-start.1
  161.4 0.0 reduce-scatter.5.cloned.1.call-start
  161.5 40.1 %all-gather.5.cloned.1.call-done = f32[1024,256]{1,0:T(8,128)} async-done(((f32[128,256]{1,0:T(8,128)}), f32[1024,256]{1,0:T(8,128)}) %all-gather.5.cloned.1.call-update) | async-done | bytes 1048592 | tf_op jit(solution)/shard_map/all_gather | solution.py:53
  201.6 4.6 %fusion = f32[512,256]{1,0:T(8,128)} fusion(f32[1024,256]{1,0:T(8,128)} %all-gather.5.cloned.1.call-done, f32[1024]{0:T(1024)S(1)} %bitcast.11, f32[512]{0:T(512)S(1)} %bitcast.17, f32[1024]{0:T(1024)S(1)} %bitcast.13, f32[512]{0:T(512)S(1)} %bitcast.19, f32[1024]{0:T(1024)S(1)} %bitcast.9, f32[512]{0:T(512)S(1)} %bitcast.15), kind=kOutput, calls=%fused_computation.1 | convolution fusion | flops 1615855616 | bytes 1591296 | tf_op jit(solution)/shard_map/while/body/eval_jaxpr/dot_general | solution.py:24
  206.2 0.0 reduce-scatter.5.cloned.1.call-update
  206.2 20.6 %reduce-scatter.5.cloned.1.call-done = f32[128,256]{1,0:T(8,128)} async-done(((f32[512,256]{1,0:T(8,128)}), f32[128,256]{1,0:T(8,128)}) %reduce-scatter.5.cloned.1.call-update) | async-done | bytes 131088 | tf_op jit(solution)/shard_map/reduce_scatter | solution.py:54
  226.8 0.0 copy-done.1
  226.8 1.0 multiply_reduce_fusion
  227.8 39.4 %psum.31 = f32[256]{0:T(256)S(1)} all-reduce(f32[256]{0:T(256)S(1)} %multiply_reduce_fusion), channel_id=1, replica_groups=mesh['row'=8,'col'=4] {'row','col'}, use_global_device_ids=true, to_apply=%region_9.10 | all-reduce | flops 256 | bytes 2048 | tf_op jit(solution)/shard_map/psum | solution.py:61
  267.2 1.7 multiply_subtract_fusion
  (5 shorter events, 0.0 us)
Async XLA Ops:
  7.2 45.9 %all-gather.3.cloned.1.call-start = ((), (), s32[]{:S(2)}) async-start(), calls=%async_computation.2 | async-start | bytes 1179648 | tf_op jit(solution)/shard_map/all_gather | solution.py:53
  7.9 70.4 %reduce-scatter.3.cloned.1.call-start = ((), (), s32[]{:S(2)}) async-start(), calls=%async_computation.3 | async-start | bytes 655360 | tf_op jit(solution)/shard_map/reduce_scatter | solution.py:54
  53.1 25.2 %copy-start = (f32[128,256]{1,0:T(8,128)S(1)}, f32[128,256]{1,0:T(8,128)}, u32[]{:S(2)}) copy-start(f32[128,256]{1,0:T(8,128)} %param.5) | copy-start | bytes 393220
  53.1 25.2 %copy-start.2 = (f32[128]{0:T(128)S(1)}, f32[128]{0:T(128)}, u32[]{:S(2)}) copy-start(f32[128]{0:T(128)} %param.4) | copy-start | bytes 1540
  57.7 143.9 %all-gather.5.cloned.1.call-start = ((), (), s32[]{:S(2)}) async-start(), calls=%async_computation.4 | async-start | bytes 1179648 | tf_op jit(solution)/shard_map/all_gather | solution.py:53
  161.4 65.3 %copy-start.1 = (f32[128,256]{1,0:T(8,128)S(1)}, f32[128,256]{1,0:T(8,128)}, u32[]{:S(2)}) copy-start(f32[128,256]{1,0:T(8,128)} %multiply_add_fusion.1) | copy-start | bytes 393220
  161.4 65.3 %reduce-scatter.5.cloned.1.call-start = ((), (), s32[]{:S(2)}) async-start(), calls=%async_computation.5 | async-start | bytes 655360 | tf_op jit(solution)/shard_map/reduce_scatter | solution.py:54
Sparse Core Ops, SparseCore 0:
  10.1 42.9 all-gather.2
  57.9 20.3 reduce-scatter.2
  161.6 40.0 all-gather.4
  206.3 20.4 reduce-scatter.4
where the time goes:
time: 276 us; the launch traced here: 275 us
  blocking collectives  153 us (55%)
  waiting for transfers between devices  93.7 us (34%)
  between operations  13.8 us (5%)
  matrix products  9.14 us (3%)
  other arithmetic  5.42 us (2%)
    psum x2, blocking collectives, squares(): return lax.psum(jnp.sum(residual * residual, axis=0), ('row', 'col'))  80.4 us
    all_gather x2, waiting for transfers between devices, body(): col_values = lax.all_gather(direction, 'row', axis=0, tiled=True)  52 us
    reduce_scatter x2, waiting for transfers between devices, body(): lax.psum_scatter(kernel_product(row_points, col_points, col_values, kerne...  41.1 us
    psum x1, blocking collectives, body(): curvature = lax.psum(jnp.sum(direction * image_vec, axis=0), ('row', 'col'))  39.4 us
    all_gather x1, blocking collectives, body(): col_points = lax.all_gather(positions, 'row', axis=1, tiled=True)  27 us
    dot_general x2, matrix products, apply_block(): jnp.dot(weights, values, preferred_element_type=jnp.float32, precision=la...  9.14 us
    all_gather x1, blocking collectives, body(): row_points = lax.all_gather(positions, 'col', axis=1, tiled=True)  6.27 us
  transfers between devices with their start and end apart: 4, of which 4 were waited for; matrix products, arithmetic and copies ran while one was open for 0% of the time, Pallas kernels for 0%

commit v1 on v0

--- a/solution.py
+++ b/solution.py
@@ -1,9 +1,26 @@
+import functools
+
 import jax
 import jax.numpy as jnp
 from jax import lax
+from jax.experimental import pallas as pl
+from jax.experimental.pallas import tpu as pltpu
 from jax.sharding import PartitionSpec as P
 
 ITERS = 2
+AXES = ("row", "col")
+F32 = jnp.float32
+BF16 = jnp.bfloat16
+LANES = 128
+EXTRA = 8
+VM = pl.BlockSpec(memory_space=pltpu.VMEM)
+KERNEL_BYTES = 32 << 20
+
+
+def constants(total):
+    kernel_scale = float(total) ** (-0.5)
+    spacing = 0.25 * float(total) ** (-1.0 / 3.0)
+    return (kernel_scale, spacing * spacing)
 
 
 def kernel_product(row_points, col_points, values, kernel_scale, softening, limit):
@@ -28,17 +45,11 @@
     return lax.map(apply_block, grouped).reshape(row_count, values.shape[1])
 
 
-def constants(total):
-    kernel_scale = float(total) ** (-0.5)
-    spacing = 0.25 * float(total) ** (-1.0 / 3.0)
-    return (kernel_scale, spacing * spacing)
-
-
 def squares(residual):
-    return lax.psum(jnp.sum(residual * residual, axis=0), ("row", "col"))
-
-
-def body(positions, radii, right_side):
+    return lax.psum(jnp.sum(residual * residual, axis=0), AXES)
+
+
+def blockwise(positions, radii, right_side):
     local_count = positions.shape[1]
     total = local_count * lax.axis_size("row") * lax.axis_size("col")
     kernel_scale, softening = constants(total)
@@ -58,7 +69,7 @@
             tiled=True,
         )
         image_vec = direction / radii[:, None] + summed
-        curvature = lax.psum(jnp.sum(direction * image_vec, axis=0), ("row", "col"))
+        curvature = lax.psum(jnp.sum(direction * image_vec, axis=0), AXES)
         step_size = norm_now / curvature
         solution = solution + step_size * direction
         residual = residual - step_size * image_vec
@@ -69,6 +80,217 @@
     return (solution, residual)
 
 
+def pack_kernel(scale, parts, pos_ref, rad_ref, rhs_ref, out_ref):
+    cols = rhs_ref.shape[1] // parts
+    flipped = rhs_ref[...].T
+    extra = jnp.concatenate(
+        [pos_ref[...] * scale, rad_ref[...], jnp.zeros((EXTRA - 4, LANES), F32)], axis=0
+    )
+    for q in range(parts):
+        out_ref[q, 0:cols, :] = flipped[q * cols : (q + 1) * cols, :]
+        out_ref[q, cols : cols + EXTRA, :] = extra
+
+
+def split(values):
+    high = values.astype(BF16)
+    return high, (values - high.astype(F32)).astype(BF16)
+
+
+def first_kernel(soft, own_ref, oth_ref, *refs):
+    pieces = (len(refs) - 4) // 2
+    highs, lows = refs[0:pieces], refs[pieces : 2 * pieces]
+    image_ref, lane_ref, sub_ref, vec_ref = refs[2 * pieces :]
+    parts, cols = own_ref.shape[0], own_ref.shape[1] - EXTRA
+    half = parts * LANES
+    for h, ref in enumerate((own_ref, oth_ref)):
+        for q in range(parts):
+            at = slice(h * half + q * LANES, h * half + (q + 1) * LANES)
+            high, low = split(ref[q, 0:cols, :])
+            vec_ref[0:cols, at] = high
+            vec_ref[cols : 2 * cols, at] = low
+            extra = ref[q, cols : cols + EXTRA, :]
+            if h == 0:
+                lane_ref[:, at] = extra
+            turned = extra.T
+            for c in range(3):
+                sub_ref[c, at, :] = jnp.broadcast_to(turned[:, c : c + 1], (LANES, LANES))
+    wide, deep, step = 512, 1024, 256
+    width = highs[0].shape[1]
+    for piece in range(pieces):
+        high_ref, low_ref = highs[piece], lows[piece]
+
+        def tile(t, _, piece=piece, high_ref=high_ref, low_ref=low_ref):
+            i0 = pl.multiple_of(t * wide, wide)
+            here = pl.ds(pl.multiple_of(piece * width + t * wide, wide), wide)
+            ends = [lane_ref[c : c + 1, here] for c in range(3)]
+
+            def rows(u, acc):
+                for r in range(0, deep, step):
+                    at = pl.ds(pl.multiple_of(u * deep + r, step), step)
+                    starts = [sub_ref[c, at, :] for c in range(3)]
+                    high, low = [], []
+                    for s in range(0, wide, LANES):
+                        gaps = [starts[c] - ends[c][:, s : s + LANES] for c in range(3)]
+                        squared = gaps[0] * gaps[0] + gaps[1] * gaps[1] + gaps[2] * gaps[2]
+                        a, b = split(lax.rsqrt(squared + soft))
+                        high.append(a)
+                        low.append(b)
+                    high, low = jnp.concatenate(high, 1), jnp.concatenate(low, 1)
+                    high_ref[at, pl.ds(i0, wide)] = high
+                    low_ref[at, pl.ds(i0, wide)] = low
+                    vec = vec_ref[:, at]
+                    acc = acc + jnp.dot(vec, high, preferred_element_type=F32)
+                    acc = acc + jnp.dot(vec, low, preferred_element_type=F32)
+                return acc
+
+            acc = lax.fori_loop(0, 2 * half // deep, rows, jnp.zeros((2 * cols, wide), F32))
+            image_ref[:, here] = acc[0:cols] + acc[cols : 2 * cols]
+            return 0
+
+        lax.fori_loop(0, width // wide, tile, 0)
+    for q in range(parts):
+        at = slice(q * LANES, (q + 1) * LANES)
+        image_ref[:, at] = image_ref[:, at] + own_ref[q, 0:cols, :] / lane_ref[3:4, at]
+
+
+def second_kernel(own_ref, oth_ref, im_own_ref, im_oth_ref, *refs):
+    pieces = (len(refs) - 5) // 2
+    highs, lows = refs[0:pieces], refs[pieces : 2 * pieces]
+    dir_ref, res_ref, image_ref, stat_ref, vec_ref = refs[2 * pieces :]
+    parts, cols = own_ref.shape[0], own_ref.shape[1] - EXTRA
+    half = parts * LANES
+    blocks = [
+        (rhs, im, q, slice(q * LANES, (q + 1) * LANES), slice(h * half + q * LANES, h * half + (q + 1) * LANES))
+        for h, (rhs, im) in enumerate(((own_ref, im_own_ref), (oth_ref, im_oth_ref)))
+        for q in range(parts)
+    ]
+    norm, curve = jnp.zeros((cols, LANES), F32), jnp.zeros((cols, LANES), F32)
+    for rhs, im, q, at, _ in blocks:
+        value = rhs[q, 0:cols, :]
+        norm = norm + value * value
+        curve = curve + value * im[:, at]
+    norm = jnp.sum(norm, axis=1, keepdims=True)
+    step = norm / jnp.sum(curve, axis=1, keepdims=True)
+    fresh = jnp.zeros((cols, LANES), F32)
+    for rhs, im, q, at, _ in blocks:
+        value = rhs[q, 0:cols, :] - step * im[:, at]
+        fresh = fresh + value * value
+    fresh = jnp.sum(fresh, axis=1, keepdims=True)
+    ratio = fresh / norm
+    for n, (rhs, im, q, at, to) in enumerate(blocks):
+        value = rhs[q, 0:cols, :]
+        left = value - step * im[:, at]
+        direction = left + ratio * value
+        if n < parts:
+            res_ref[:, at] = left
+            dir_ref[:, at] = direction
+        high, low = split(direction)
+        vec_ref[0:cols, to] = high
+        vec_ref[cols : 2 * cols, to] = low
+    width = highs[0].shape[1]
+    deep = 256
+    for piece in range(pieces):
+        acc = jnp.zeros((2 * cols, width), F32)
+        for r in range(0, 2 * half, deep):
+            vec = vec_ref[:, r : r + deep]
+            acc = acc + jnp.dot(vec, highs[piece][r : r + deep, :], preferred_element_type=F32)
+            acc = acc + jnp.dot(vec, lows[piece][r : r + deep, :], preferred_element_type=F32)
+        image_ref[:, piece * width : (piece + 1) * width] = acc[0:cols] + acc[cols : 2 * cols]
+    curve = jnp.zeros((cols, LANES), F32)
+    for q in range(parts):
+        at = slice(q * LANES, (q + 1) * LANES)
+        direction = dir_ref[:, at]
+        image = image_ref[:, at] + direction / own_ref[q, cols + 3 : cols + 4, :]
+        image_ref[:, at] = image
+        curve = curve + direction * image
+    stat_ref[0] = curve
+    stat_ref[1] = jnp.broadcast_to(step, (cols, LANES))
+    stat_ref[2] = jnp.broadcast_to(fresh, (cols, LANES))
+
+
+def last_kernel(own_ref, dir_ref, res_ref, image_ref, stat_ref, curve_ref, out_ref):
+    parts, cols = own_ref.shape[0], own_ref.shape[1] - EXTRA
+    curve = jnp.sum(stat_ref[0] + curve_ref[...], axis=1, keepdims=True)
+    first = stat_ref[1, :, 0:1]
+    step = stat_ref[2, :, 0:1] / curve
+    for q in range(parts):
+        at = slice(q * LANES, (q + 1) * LANES)
+        out_ref[q, 0:cols, :] = first * own_ref[q, 0:cols, :] + step * dir_ref[:, at]
+        out_ref[q, cols : 2 * cols, :] = res_ref[:, at] - step * image_ref[:, at]
+
+
+def unpack_kernel(in_ref, sol_ref, res_ref):
+    parts, cols = in_ref.shape[0], in_ref.shape[1] // 2
+    sol_ref[...] = in_ref[:, 0:cols, :].reshape(parts * cols, LANES).T
+    res_ref[...] = in_ref[:, cols : 2 * cols, :].reshape(parts * cols, LANES).T
+
+
+def shape(*dims, dtype=F32):
+    return jax.ShapeDtypeStruct(dims, dtype)
+
+
+def call(kernel, out, count, scratch=(), limit=16):
+    many = isinstance(out, (list, tuple))
+    return pl.pallas_call(
+        kernel,
+        out_shape=out,
+        in_specs=[VM] * count,
+        out_specs=[VM] * len(out) if many else VM,
+        scratch_shapes=list(scratch),
+        compiler_params=pltpu.CompilerParams(vmem_limit_bytes=limit << 20),
+    )
+
+
+def by_columns(positions, radii, right_side):
+    row_size, col_size = lax.axis_size("row"), lax.axis_size("col")
+    devices = row_size * col_size
+    parts = devices // 2
+    total = right_side.shape[0] * devices
+    cols = right_side.shape[1] // parts
+    half = total // 2
+    kernel_scale, softening = constants(total)
+    soft = softening / (kernel_scale * kernel_scale)
+    groups = [[2 * chip + core for chip in range(parts)] for core in range(2)]
+    swap = [(i, i ^ 1) for i in range(col_size)]
+    pieces = 2
+
+    packed = call(functools.partial(pack_kernel, 1.0 / kernel_scale, parts), shape(parts, cols + EXTRA, LANES), 3)(
+        positions, radii.reshape(1, -1), right_side
+    )
+    own = lax.all_to_all(packed, AXES, 0, 0, axis_index_groups=groups, tiled=True)
+    oth = lax.ppermute(own, "col", swap)
+    *kernel, image = call(
+        functools.partial(first_kernel, soft),
+        [shape(total, half // pieces, dtype=BF16)] * (2 * pieces) + [shape(cols, half)],
+        2,
+        [
+            pltpu.VMEM((EXTRA, half), F32),
+            pltpu.VMEM((3, total, LANES), F32),
+            pltpu.VMEM((2 * cols, total), BF16),
+        ],
+    )(own, oth)
+    direction, residual, image, stats = call(
+        second_kernel,
+        [shape(cols, half)] * 3 + [shape(3, cols, LANES)],
+        4 + 2 * pieces,
+        [pltpu.VMEM((2 * cols, total), BF16)],
+    )(own, oth, image, lax.ppermute(image, "col", swap), *kernel)
+    curve = lax.ppermute(stats[0], "col", swap)
+    mixed = call(last_kernel, shape(parts, 2 * cols, LANES), 6)(own, direction, residual, image, stats, curve)
+    mixed = lax.all_to_all(mixed, AXES, 0, 0, axis_index_groups=groups, tiled=True)
+    return tuple(call(unpack_kernel, [shape(LANES, parts * cols)] * 2, 1)(mixed))
+
+
+def body(positions, radii, right_side):
+    devices = lax.axis_size("row") * lax.axis_size("col")
+    rows, columns = right_side.shape
+    total = rows * devices
+    fits = rows == LANES and devices % 2 == 0 and columns % (devices // 2) == 0
+    if fits and columns // (devices // 2) == 16 and 2 * total * total <= KERNEL_BYTES:
+        return by_columns(positions, radii, right_side)
+    return blockwise(positions, radii, right_side)
+
+
 def solution(mesh):
     return jax.shard_map(
         body,

time: 276 us -> 65 us (0.24)
  blocking collectives: 153 us -> 30.1 us
  waiting for transfers between devices: 93.7 us -> 3.67 us
  Pallas kernels: 0 us -> 27.7 us
  between operations: 13.8 us -> 0.68 us
  matrix products: 9.14 us -> 0 us
  other arithmetic: 5.42 us -> 0 us
    psum x3 -> x0, blocking collectives: 120 us -> none  [the longest x2 80.4 us: squares(): return lax.psum(jnp.sum(residual * residual, axis=0), ('row', 'col'))]
    all_gather x2 -> x0, waiting for transfers between devices: 52 us -> none  [body(): col_values = lax.all_gather(direction, 'row', axis=0, tiled=True)]
    reduce_scatter x2 -> x0, waiting for transfers between devices: 41.1 us -> none  [body(): lax.psum_scatter(kernel_product(row_points, col_points, col_values, kerne...]
    all_gather x2 -> x0, blocking collectives: 33.3 us -> none  [the longest x1 27 us: body(): col_points = lax.all_gather(positions, 'row', axis=1, tiled=True)]
    all_to_all x0 -> x2, blocking collectives: none -> 30.1 us  [the longest x1 16.8 us: by_columns(): lax.all_to_all(packed, AXES, 0, 0, axis_index_groups=groups, tiled=True)]
    pallas_call x0 -> x5, Pallas kernels: none -> 27.7 us  [the longest x1 20.7 us: by_columns(): call(functools.partial(first_kernel, soft), [shape(total, half // pieces,...]
    dot_general x2 -> x0, matrix products: 9.14 us -> none  [apply_block(): jnp.dot(weights, values, preferred_element_type=jnp.float32, precision=la...]
    ppermute x0 -> x3, waiting for transfers between devices: none -> 3.67 us  [the longest x1 1.44 us: by_columns(): oth = lax.ppermute(own, 'col', swap)]
  transfers between devices with their start and end apart: 4 -> 3, of which waited for: 4 -> 3; matrix products, arithmetic and copies ran while one was open for 0% -> 0% of each run, Pallas kernels for 0% -> 0%
where the time goes in v1:
time: 65 us; the launch traced here: 64.8 us
  blocking collectives  30.1 us (46%)
  Pallas kernels  27.7 us (43%)
  waiting for transfers between devices  3.67 us (6%)
  local copies, waits for them, and re-layouts  2.24 us (3%)
  between operations  0.68 us (1%)
    pallas_call x1, Pallas kernels, by_columns(): call(functools.partial(first_kernel, soft), [shape(total, half // pieces,...  20.7 us
    all_to_all x1, blocking collectives, by_columns(): lax.all_to_all(packed, AXES, 0, 0, axis_index_groups=groups, tiled=True)  16.8 us
    all_to_all x1, blocking collectives, by_columns(): lax.all_to_all(mixed, AXES, 0, 0, axis_index_groups=groups, tiled=True)  13.4 us
    pallas_call x1, Pallas kernels, by_columns(): call(second_kernel, [shape(cols, half)] * 3 + [shape(3, cols, LANES)], 4...  5.9 us
    unnamed x6, local copies, waits for them, and re-layouts  2.23 us
    ppermute x1, waiting for transfers between devices, by_columns(): oth = lax.ppermute(own, 'col', swap)  1.44 us
  transfers between devices with their start and end apart: 3, of which 3 were waited for; matrix products, arithmetic and copies ran while one was open for 0% of the time, Pallas kernels for 0%

profile of v1, /device:TPU:0, one launch (start us, length us, event | category | flops | bytes accessed | tf_op | source)
XLA Modules:
  0.0 64.8 jit_solution(13965756958901748216)
XLA Ops:
  0.6 0.0 copy-start
  0.6 0.9 %copy-done = f32[128,256]{1,0:T(8,128)S(1)} copy-done((f32[128,256]{1,0:T(8,128)S(1)}, f32[128,256]{1,0:T(8,128)}, u32[]{:S(2)}) %copy-start) | copy-done | bytes 131096
  1.5 0.0 copy-start.1
  1.5 0.7 %copy-done.1 = f32[3,128]{1,0:T(4,128)S(1)} copy-done((f32[3,128]{1,0:T(4,128)S(1)}, f32[3,128]{1,0:T(4,128)}, u32[]{:S(2)}) %copy-start.1) | copy-done | bytes 1560
  2.2 0.0 copy-start.2
  2.2 0.7 %copy-done.2 = f32[128]{0:T(128)S(1)} copy-done((f32[128]{0:T(128)S(1)}, f32[128]{0:T(128)}, u32[]{:S(2)}) %copy-start.2) | copy-done | bytes 536
  2.9 0.1 shard_map.50
  3.0 16.8 %all_to_all.10.own_ref = f32[16,24,128]{2,1,0:T(8,128)S(1)} all-to-all(f32[16,24,128]{2,1,0:T(8,128)S(1)} %shard_map.50), channel_id=1, replica_groups={{0,2,4,6,8,10,12,14,16,18,20,22,24,26,28,30},{1,3,5,7,9,11,13,15,17,19,..., dimensions={0} | all-to-all | bytes 393216 | tf_op jit(solution)/shard_map/all_to_all | solution.py:260
  19.7 0.0 collective-permute-start
  19.7 1.4 %collective-permute-done.oth_ref = f32[16,24,128]{2,1,0:T(8,128)S(1)} collective-permute-done((f32[16,24,128]{2,1,0:T(8,128)S(1)}, f32[16,24,128]{2,1,0:T(8,128)S(1)}, u32[]{:S(2)}, u32[]{:S(2)}) %collective-permute-start) | collective-permute-done | bytes 196640 | tf_op jit(solution)/shard_map/ppermute | solution.py:261
  21.2 20.7 %shard_map.51 = (bf16[4096,1024]{1,0:T(8,128)(2,1)S(1)}, bf16[4096,1024]{1,0:T(8,128)(2,1)S(1)}, bf16[4096,1024]{1,0:T(8,128)(2,1)S(1)}, bf16[4096,1024]{1,0:T(8,128)(2,1)S(1)}, f32[16,2048]{1,0:T(8,128)S(1)}) custom-call(f32[16,24,128]{2,1,0:T(8,128)S(1)} %all_to_all.10.own_ref, f32[16,24,128]{2,1,0:T(8,128)S(1)} %collective-permute-done.oth_ref), custom_call_target="tpu_custom_call" | custom-call | tf_op jit(solution)/shard_map/pallas_call | solution.py:262
  41.9 0.2 collective-permute-start.1
  42.1 1.2 %collective-permute-done.1.im_oth_ref = f32[16,2048]{1,0:T(8,128)S(1)} collective-permute-done((f32[16,2048]{1,0:T(8,128)S(1)}, f32[16,2048]{1,0:T(8,128)S(1)}, u32[]{:S(2)}, u32[]{:S(2)}) %collective-permute-start.1) | collective-permute-done | bytes 131104 | tf_op jit(solution)/shard_map/ppermute | solution.py:277
  43.3 5.9 %shard_map.52 = (f32[16,2048]{1,0:T(8,128)S(1)}, f32[16,2048]{1,0:T(8,128)S(1)}, f32[16,2048]{1,0:T(8,128)S(1)}, f32[3,16,128]{2,1,0:T(8,128)S(1)}) custom-call(f32[16,24,128]{2,1,0:T(8,128)S(1)} %all_to_all.10.own_ref, f32[16,24,128]{2,1,0:T(8,128)S(1)} %collective-permute-done.oth_ref, f32[16,2048]{1,0:T(8,128)S(1)} %get-tuple-element.11.im_own_ref, ...), custom_call_target="tpu_custom_call" | custom-call | tf_op jit(solution)/shard_map/pallas_call | solution.py:272
  49.2 0.2 collective-permute-start.2
  49.4 1.0 %collective-permute-done.2.curve_ref = f32[16,128]{1,0:T(8,128)S(1)} collective-permute-done((f32[16,128]{1,0:T(8,128)S(1)}, f32[16,128]{1,0:T(8,128)S(1)}, u32[]{:S(2)}, u32[]{:S(2)}) %collective-permute-start.2) | collective-permute-done | bytes 8224 | tf_op jit(solution)/shard_map/ppermute | solution.py:278
  50.4 0.2 shard_map.53
  50.6 13.4 %all_to_all.11.in_ref = f32[16,32,128]{2,1,0:T(8,128)S(1)} all-to-all(f32[16,32,128]{2,1,0:T(8,128)S(1)} %shard_map.53), channel_id=1, replica_groups={{0,2,4,6,8,10,12,14,16,18,20,22,24,26,28,30},{1,3,5,7,9,11,13,15,17,19,..., dimensions={0} | all-to-all | bytes 524288 | tf_op jit(solution)/shard_map/all_to_all | solution.py:280
  64.0 0.8 %shard_map.54 = (f32[128,256]{1,0:T(8,128)}, f32[128,256]{1,0:T(8,128)}) custom-call(f32[16,32,128]{2,1,0:T(8,128)S(1)} %all_to_all.11.in_ref), custom_call_target="tpu_custom_call" | custom-call | tf_op jit(solution)/shard_map/pallas_call | solution.py:281
  (1 shorter events, 0.0 us)
Async XLA Ops:
  0.6 0.9 %copy-start = (f32[128,256]{1,0:T(8,128)S(1)}, f32[128,256]{1,0:T(8,128)}, u32[]{:S(2)}) copy-start(f32[128,256]{1,0:T(8,128)} %rhs_ref.1) | copy-start | bytes 393220
  1.5 0.7 %copy-start.1 = (f32[3,128]{1,0:T(4,128)S(1)}, f32[3,128]{1,0:T(4,128)}, u32[]{:S(2)}) copy-start(f32[3,128]{1,0:T(4,128)} %pos_ref.1) | copy-start | bytes 4612
  2.2 0.7 %copy-start.2 = (f32[128]{0:T(128)S(1)}, f32[128]{0:T(128)}, u32[]{:S(2)}) copy-start(f32[128]{0:T(128)} %param.4) | copy-start | bytes 1540
  19.7 1.4 %collective-permute-start = (f32[16,24,128]{2,1,0:T(8,128)S(1)}, f32[16,24,128]{2,1,0:T(8,128)S(1)}, u32[]{:S(2)}, u32[]{:S(2)}) collective-permute-start(f32[16,24,128]{2,1,0:T(8,128)S(1)} %all_to_all.10.own_ref), channel_id=1, source_target_pairs={{0,1},{1,0},{2,3},{3,2},{4,5},{5,4},{6,7},{7,6},{8,9},{9,8},{10,11... | collective-permute-start | bytes 589832 | tf_op jit(solution)/shard_map/ppermute | solution.py:261
  41.9 1.4 %collective-permute-start.1 = (f32[16,2048]{1,0:T(8,128)S(1)}, f32[16,2048]{1,0:T(8,128)S(1)}, u32[]{:S(2)}, u32[]{:S(2)}) collective-permute-start(f32[16,2048]{1,0:T(8,128)S(1)} %get-tuple-element.11.im_own_ref), channel_id=1, source_target_pairs={{0,1},{1,0},{2,3},{3,2},{4,5},{5,4},{6,7},{7,6},{8,9},{9,8},{10,11... | collective-permute-start | bytes 393224 | tf_op jit(solution)/shard_map/ppermute | solution.py:277
  49.2 1.2 %collective-permute-start.2 = (f32[16,128]{1,0:T(8,128)S(1)}, f32[16,128]{1,0:T(8,128)S(1)}, u32[]{:S(2)}, u32[]{:S(2)}) collective-permute-start(f32[16,128]{1,0:T(8,128)S(1)} %slice_bitcast_fusion), channel_id=1, source_target_pairs={{0,1},{1,0},{2,3},{3,2},{4,5},{5,4},{6,7},{7,6},{8,9},{9,8},{10,11... | collective-permute-start | bytes 24584 | tf_op jit(solution)/shard_map/ppermute | solution.py:278

commit v2 on v0

--- a/solution.py
+++ b/solution.py
@@ -1,9 +1,29 @@
+import functools
+
 import jax
 import jax.numpy as jnp
 from jax import lax
+from jax.experimental import pallas as pl
+from jax.experimental.pallas import tpu as pltpu
 from jax.sharding import PartitionSpec as P
 
 ITERS = 2
+AXES = ("row", "col")
+F32 = jnp.float32
+BF16 = jnp.bfloat16
+LANES = 128
+EXTRA = 8
+PANEL = 256
+WIDE = 512
+VM = pl.BlockSpec(memory_space=pltpu.VMEM)
+SM = pl.BlockSpec(memory_space=pltpu.SMEM)
+KERNEL_BYTES = 32 << 20
+
+
+def constants(total):
+    kernel_scale = float(total) ** (-0.5)
+    spacing = 0.25 * float(total) ** (-1.0 / 3.0)
+    return (kernel_scale, spacing * spacing)
 
 
 def kernel_product(row_points, col_points, values, kernel_scale, softening, limit):
@@ -28,17 +48,11 @@
     return lax.map(apply_block, grouped).reshape(row_count, values.shape[1])
 
 
-def constants(total):
-    kernel_scale = float(total) ** (-0.5)
-    spacing = 0.25 * float(total) ** (-1.0 / 3.0)
-    return (kernel_scale, spacing * spacing)
-
-
 def squares(residual):
-    return lax.psum(jnp.sum(residual * residual, axis=0), ("row", "col"))
-
-
-def body(positions, radii, right_side):
+    return lax.psum(jnp.sum(residual * residual, axis=0), AXES)
+
+
+def blockwise(positions, radii, right_side):
     local_count = positions.shape[1]
     total = local_count * lax.axis_size("row") * lax.axis_size("col")
     kernel_scale, softening = constants(total)
@@ -58,7 +72,7 @@
             tiled=True,
         )
         image_vec = direction / radii[:, None] + summed
-        curvature = lax.psum(jnp.sum(direction * image_vec, axis=0), ("row", "col"))
+        curvature = lax.psum(jnp.sum(direction * image_vec, axis=0), AXES)
         step_size = norm_now / curvature
         solution = solution + step_size * direction
         residual = residual - step_size * image_vec
@@ -69,6 +83,321 @@
     return (solution, residual)
 
 
+def pack_kernel(scale, parts, pos_hbm, rad_hbm, rhs_hbm, out_ref, pos_ref, rad_ref, rhs_ref, sems):
+    copies = [
+        pltpu.make_async_copy(src, dst, sems.at[n])
+        for n, (src, dst) in enumerate(((rhs_hbm, rhs_ref), (pos_hbm, pos_ref), (rad_hbm, rad_ref)))
+    ]
+    for copy in copies:
+        copy.start()
+    for copy in copies:
+        copy.wait()
+    cols = rhs_ref.shape[1] // parts
+    flipped = rhs_ref[...].T
+    extra = jnp.concatenate(
+        [pos_ref[...] * scale, rad_ref[...], jnp.zeros((EXTRA - 4, LANES), F32)], axis=0
+    )
+    for q in range(parts):
+        out_ref[q, 0:cols, :] = flipped[q * cols : (q + 1) * cols, :]
+        out_ref[q, cols : cols + EXTRA, :] = extra
+
+
+def split(values):
+    high = values.astype(BF16)
+    return high, (values - high.astype(F32)).astype(BF16)
+
+
+def product(vec, high, low):
+    return jnp.dot(vec, high, preferred_element_type=F32) + jnp.dot(vec, low, preferred_element_type=F32)
+
+
+def evaluate(soft, sub_ref, rows, lane_ref, at):
+    starts = [sub_ref[c, rows, :] for c in range(3)]
+    ends = [lane_ref[c : c + 1, at] for c in range(3)]
+    high, low = [], []
+    for s in range(0, ends[0].shape[1], LANES):
+        gaps = [starts[c] - ends[c][:, s : s + LANES] for c in range(3)]
+        squared = gaps[0] * gaps[0] + gaps[1] * gaps[1] + gaps[2] * gaps[2]
+        a, b = split(lax.rsqrt(squared + soft))
+        high.append(a)
+        low.append(b)
+    return jnp.concatenate(high, 1), jnp.concatenate(low, 1)
+
+
+def unpack(ref, lane_ref, vec_ref, sub_ref=None):
+    parts, cols = ref.shape[0], ref.shape[1] - EXTRA
+    for q in range(parts):
+        at = slice(q * LANES, (q + 1) * LANES)
+        high, low = split(ref[q, 0:cols, :])
+        vec_ref[0:cols, at] = high
+        vec_ref[cols : 2 * cols, at] = low
+        extra = ref[q, cols : cols + EXTRA, :]
+        lane_ref[:, at] = extra
+        if sub_ref is not None:
+            turned = extra.T
+            for c in range(3):
+                sub_ref[c, at, :] = jnp.broadcast_to(turned[:, c : c + 1], (LANES, LANES))
+
+
+def near_spans(panels):
+    spans, start = [], 0
+    for t in range(panels):
+        spans.append((t, slice(t * PANEL, panels * PANEL), start))
+        start += (panels - t) * PANEL
+    return spans
+
+
+def across_spans(panels):
+    spans, start = [], 0
+    for t in range(1, panels):
+        spans.append((t, slice(0, t * PANEL), start))
+        start += t * PANEL
+    return spans
+
+
+def first_kernel(soft, own_ref, high_ref, low_ref, high_t_ref, low_t_ref, vec_ref, sub_ref, acc_ref, lane_ref):
+    panels = vec_ref.shape[1] // PANEL
+    unpack(own_ref, lane_ref, vec_ref, sub_ref)
+    acc_ref[...] = jnp.zeros_like(acc_ref)
+    for t, columns, start in near_spans(panels):
+        rows = slice(t * PANEL, (t + 1) * PANEL)
+        for c in range(columns.start, columns.stop, WIDE):
+            at = slice(c, min(c + WIDE, columns.stop))
+            high, low = evaluate(soft, sub_ref, rows, lane_ref, at)
+            to = start + c - columns.start
+            high_ref[:, to : to + at.stop - c] = high
+            low_ref[:, to : to + at.stop - c] = low
+            acc_ref[:, at] += product(vec_ref[:, rows], high, low)
+            skip = PANEL if c == columns.start else 0
+            if at.stop - c > skip:
+                high, low = high[:, skip:].T, low[:, skip:].T
+                to = to + skip - (t + 1) * PANEL
+                high_t_ref[to : to + at.stop - c - skip, :] = high
+                low_t_ref[to : to + at.stop - c - skip, :] = low
+                acc_ref[:, rows] += product(vec_ref[:, c + skip : at.stop], high, low)
+
+
+def middle_kernel(soft, core_ref, own_ref, oth_ref, vec_ref, sub_ref, near_ref, *refs):
+    high_ref, low_ref, high_t_ref, low_t_ref, far_ref, image_ref, acc_ref, lane_ref, vec_oth_ref = refs
+    parts, cols = own_ref.shape[0], own_ref.shape[1] - EXTRA
+    half = parts * LANES
+    panels = half // PANEL
+    unpack(oth_ref, lane_ref, vec_oth_ref)
+    acc_ref[:, 0:half] = near_ref[...]
+    acc_ref[:, half:] = jnp.zeros_like(near_ref)
+    for t, columns, start in across_spans(panels):
+        rows = slice(t * PANEL, (t + 1) * PANEL)
+        for c in range(columns.start, columns.stop, WIDE):
+            at = slice(c, min(c + WIDE, columns.stop))
+            high, low = evaluate(soft, sub_ref, rows, lane_ref, at)
+            to = slice(start + c, start + at.stop)
+            high_ref[:, to] = high
+            low_ref[:, to] = low
+            acc_ref[:, half + c : half + at.stop] += product(vec_ref[:, rows], high, low)
+            high, low = high.T, low.T
+            high_t_ref[to, :] = high
+            low_t_ref[to, :] = low
+            acc_ref[:, rows] += product(vec_oth_ref[:, at], high, low)
+    for n in range(panels // 2):
+        place = pl.multiple_of((core_ref[0] * (panels // 2) + n) * PANEL, PANEL)
+        rows, at = pl.ds(place, PANEL), pl.ds(pl.multiple_of(half + place, PANEL), PANEL)
+        high, low = evaluate(soft, sub_ref, rows, lane_ref, rows)
+        far_ref[n, 0] = high
+        far_ref[n, 1] = low
+        acc_ref[:, at] += product(vec_ref[:, rows], high, low)
+        high, low = high.T, low.T
+        far_ref[n, 2] = high
+        far_ref[n, 3] = low
+        acc_ref[:, rows] += product(vec_oth_ref[:, rows], high, low)
+    for q in range(parts):
+        at = slice(q * LANES, (q + 1) * LANES)
+        here = own_ref[q, 0:cols, :] / own_ref[q, cols + 3 : cols + 4, :]
+        image_ref[:, at] = acc_ref[0:cols, at] + acc_ref[cols : 2 * cols, at] + here
+    image_ref[:, half:] = acc_ref[0:cols, half:] + acc_ref[cols : 2 * cols, half:]
+
+
+def second_kernel(core_ref, own_ref, oth_ref, mine_ref, theirs_ref, *refs):
+    near, across, far_ref = refs[0:4], refs[4:8], refs[8]
+    dir_ref, res_ref, image_ref, send_ref, stat_ref, vec_ref, acc_ref, sum_ref = refs[9:]
+    parts, cols = own_ref.shape[0], own_ref.shape[1] - EXTRA
+    half = parts * LANES
+    panels = half // PANEL
+    sum_ref[:, 0:half] = mine_ref[:, 0:half] + theirs_ref[:, half:]
+    sum_ref[:, half:] = mine_ref[:, half:] + theirs_ref[:, 0:half]
+    blocks = [
+        (ref, q, slice(h * half + q * LANES, h * half + (q + 1) * LANES))
+        for h, ref in enumerate((own_ref, oth_ref))
+        for q in range(parts)
+    ]
+    zero = jnp.zeros((cols, LANES), F32)
+    norm, curve, fresh = zero, zero, zero
+    for ref, q, at in blocks:
+        value = ref[q, 0:cols, :]
+        norm = norm + value * value
+        curve = curve + value * sum_ref[:, at]
+    norm = jnp.sum(norm, axis=1, keepdims=True)
+    step = norm / jnp.sum(curve, axis=1, keepdims=True)
+    for ref, q, at in blocks:
+        value = ref[q, 0:cols, :] - step * sum_ref[:, at]
+        fresh = fresh + value * value
+    fresh = jnp.sum(fresh, axis=1, keepdims=True)
+    ratio = fresh / norm
+    for n, (ref, q, at) in enumerate(blocks):
+        value = ref[q, 0:cols, :]
+        left = value - step * sum_ref[:, at]
+        direction = left + ratio * value
+        if n < parts:
+            res_ref[:, at] = left
+        dir_ref[:, at] = direction
+        high, low = split(direction)
+        vec_ref[0:cols, at] = high
+        vec_ref[cols : 2 * cols, at] = low
+    acc_ref[...] = jnp.zeros_like(acc_ref)
+    for t, columns, start in near_spans(panels):
+        rows, after = slice(t * PANEL, (t + 1) * PANEL), slice((t + 1) * PANEL, half)
+        to = slice(start, start + half - rows.start)
+        acc_ref[:, columns] += product(vec_ref[:, rows], near[0][:, to], near[1][:, to])
+        if after.start < half:
+            to = slice(start - rows.start, start - rows.start + half - after.start)
+            acc_ref[:, rows] += product(vec_ref[:, after], near[2][to, :], near[3][to, :])
+    for t, columns, start in across_spans(panels):
+        rows, there = slice(t * PANEL, (t + 1) * PANEL), slice(half, half + columns.stop)
+        to = slice(start, start + columns.stop)
+        acc_ref[:, there] += product(vec_ref[:, rows], across[0][:, to], across[1][:, to])
+        acc_ref[:, rows] += product(vec_ref[:, there], across[2][to, :], across[3][to, :])
+    for n in range(panels // 2):
+        place = pl.multiple_of((core_ref[0] * (panels // 2) + n) * PANEL, PANEL)
+        rows, at = pl.ds(place, PANEL), pl.ds(pl.multiple_of(half + place, PANEL), PANEL)
+        acc_ref[:, at] += product(vec_ref[:, rows], far_ref[n, 0], far_ref[n, 1])
+        acc_ref[:, rows] += product(vec_ref[:, at], far_ref[n, 2], far_ref[n, 3])
+    curve = zero
+    for n, (ref, q, at) in enumerate(blocks):
+        direction = dir_ref[:, at]
+        image = acc_ref[0:cols, at] + acc_ref[cols : 2 * cols, at]
+        if n < parts:
+            image = image + direction / own_ref[q, cols + 3 : cols + 4, :]
+            image_ref[:, at] = image
+        else:
+            send_ref[:, at.start - half : at.stop - half] = image
+        curve = curve + direction * image
+    send_ref[:, half:] = curve
+    stat_ref[0] = jnp.broadcast_to(step, (cols, LANES))
+    stat_ref[1] = jnp.broadcast_to(fresh, (cols, LANES))
+
+
+def last_kernel(own_ref, dir_ref, res_ref, image_ref, send_ref, come_ref, stat_ref, out_ref):
+    parts, cols = own_ref.shape[0], own_ref.shape[1] - EXTRA
+    half = parts * LANES
+    curve = jnp.sum(send_ref[:, half:] + come_ref[:, half:], axis=1, keepdims=True)
+    first = stat_ref[0, :, 0:1]
+    step = stat_ref[1, :, 0:1] / curve
+    for q in range(parts):
+        at = slice(q * LANES, (q + 1) * LANES)
+        out_ref[q, 0:cols, :] = first * own_ref[q, 0:cols, :] + step * dir_ref[:, at]
+        out_ref[q, cols : 2 * cols, :] = res_ref[:, at] - step * (image_ref[:, at] + come_ref[:, at])
+
+
+def unpack_kernel(in_ref, sol_ref, res_ref):
+    parts, cols = in_ref.shape[0], in_ref.shape[1] // 2
+    sol_ref[...] = in_ref[:, 0:cols, :].reshape(parts * cols, LANES).T
+    res_ref[...] = in_ref[:, cols : 2 * cols, :].reshape(parts * cols, LANES).T
+
+
+def shape(*dims, dtype=F32):
+    return jax.ShapeDtypeStruct(dims, dtype)
+
+
+def call(kernel, out, ins, scratch=(), limit=8):
+    return pl.pallas_call(
+        kernel,
+        out_shape=out,
+        in_specs=ins,
+        out_specs=[VM] * len(out),
+        scratch_shapes=list(scratch),
+        compiler_params=pltpu.CompilerParams(vmem_limit_bytes=limit << 20),
+    )
+
+
+def by_columns(positions, radii, right_side):
+    row_size, col_size = lax.axis_size("row"), lax.axis_size("col")
+    devices = row_size * col_size
+    parts = devices // 2
+    rows, columns = right_side.shape
+    total = rows * devices
+    cols = columns // parts
+    half = total // 2
+    panels = half // PANEL
+    kernel_scale, softening = constants(total)
+    soft = softening / (kernel_scale * kernel_scale)
+    groups = [[2 * chip + core for chip in range(parts)] for core in range(2)]
+    swap = [(i, i ^ 1) for i in range(col_size)]
+    core = (lax.axis_index("col") % 2).astype(jnp.int32).reshape(1)
+
+    (packed,) = call(
+        functools.partial(pack_kernel, 1.0 / kernel_scale, parts),
+        [shape(parts, cols + EXTRA, LANES)],
+        [pl.BlockSpec(memory_space=pltpu.HBM)] * 3,
+        [
+            pltpu.VMEM((3, LANES), F32),
+            pltpu.VMEM((1, LANES), F32),
+            pltpu.VMEM((LANES, columns), F32),
+            pltpu.SemaphoreType.DMA((3,)),
+        ],
+        60,
+    )(positions, radii.reshape(1, -1), right_side)
+    own = lax.all_to_all(packed, AXES, 0, 0, axis_index_groups=groups, tiled=True)
+    oth = lax.ppermute(own, "col", swap)
+    sizes = [sum(cs.stop - cs.start for _, cs, _ in spans(panels)) for spans in (near_spans, across_spans)]
+    *near, vec, sub, acc = call(
+        functools.partial(first_kernel, soft),
+        [shape(PANEL, sizes[0], dtype=BF16)] * 2
+        + [shape(sizes[0] - half, PANEL, dtype=BF16)] * 2
+        + [shape(2 * cols, half, dtype=BF16), shape(3, half, LANES), shape(2 * cols, half)],
+        [VM],
+        [pltpu.VMEM((EXTRA, half), F32)],
+        16,
+    )(own)
+    *across, mine = call(
+        functools.partial(middle_kernel, soft),
+        [shape(PANEL, sizes[1], dtype=BF16)] * 2
+        + [shape(sizes[1], PANEL, dtype=BF16)] * 2
+        + [shape(panels // 2, 4, PANEL, PANEL, dtype=BF16), shape(cols, total)],
+        [SM] + [VM] * 5,
+        [
+            pltpu.VMEM((2 * cols, total), F32),
+            pltpu.VMEM((EXTRA, half), F32),
+            pltpu.VMEM((2 * cols, half), BF16),
+        ],
+        16,
+    )(core, own, oth, vec, sub, acc)
+    direction, residual, image, send, stats = call(
+        second_kernel,
+        [shape(cols, total), shape(cols, half), shape(cols, half), shape(cols, half + LANES), shape(2, cols, LANES)],
+        [SM] + [VM] * 13,
+        [
+            pltpu.VMEM((2 * cols, total), BF16),
+            pltpu.VMEM((2 * cols, total), F32),
+            pltpu.VMEM((cols, total), F32),
+        ],
+    )(core, own, oth, mine, lax.ppermute(mine, "col", swap), *near, *across)
+    come = lax.ppermute(send, "col", swap)
+    (mixed,) = call(last_kernel, [shape(parts, 2 * cols, LANES)], [VM] * 7)(
+        own, direction, residual, image, send, come, stats
+    )
+    mixed = lax.all_to_all(mixed, AXES, 0, 0, axis_index_groups=groups, tiled=True)
+    return tuple(call(unpack_kernel, [shape(LANES, columns)] * 2, [VM])(mixed))
+
+
+def body(positions, radii, right_side):
+    devices = lax.axis_size("row") * lax.axis_size("col")
+    rows, columns = right_side.shape
+    total = rows * devices
+    fits = rows == LANES and total % (4 * PANEL) == 0 and 16 * devices == 2 * columns
+    if fits and 2 * total * total <= KERNEL_BYTES:
+        return by_columns(positions, radii, right_side)
+    return blockwise(positions, radii, right_side)
+
+
 def solution(mesh):
     return jax.shard_map(
         body,

time: 276 us -> 66.6 us (0.24)
  blocking collectives: 153 us -> 30.5 us
  waiting for transfers between devices: 93.7 us -> 2.16 us
  Pallas kernels: 0 us -> 20.3 us
  between operations: 13.8 us -> 0.69 us
  local copies, waits for them, and re-layouts: 0.03 us -> 11.7 us
  matrix products: 9.14 us -> 0 us
  other arithmetic: 5.42 us -> 0 us
    psum x3 -> x0, blocking collectives: 120 us -> none  [the longest x2 80.4 us: squares(): return lax.psum(jnp.sum(residual * residual, axis=0), ('row', 'col'))]
    all_gather x2 -> x0, waiting for transfers between devices: 52 us -> none  [body(): col_values = lax.all_gather(direction, 'row', axis=0, tiled=True)]
    reduce_scatter x2 -> x0, waiting for transfers between devices: 41.1 us -> none  [body(): lax.psum_scatter(kernel_product(row_points, col_points, col_values, kerne...]
    all_gather x2 -> x0, blocking collectives: 33.3 us -> none  [the longest x1 27 us: body(): col_points = lax.all_gather(positions, 'row', axis=1, tiled=True)]
    all_to_all x0 -> x2, blocking collectives: none -> 30.5 us  [the longest x1 17 us: by_columns(): lax.all_to_all(packed, AXES, 0, 0, axis_index_groups=groups, tiled=True)]
    pallas_call x0 -> x6, Pallas kernels: none -> 20.3 us  [the longest x1 6.44 us: by_columns(): call(second_kernel, [shape(cols, total), shape(cols, half), shape(cols, h...]
    unnamed x6 -> x12, local copies, waits for them, and re-layouts: 0.01 us -> 11.7 us
    dot_general x2 -> x0, matrix products: 9.14 us -> none  [apply_block(): jnp.dot(weights, values, preferred_element_type=jnp.float32, precision=la...]
  transfers between devices with their start and end apart: 4 -> 3, of which waited for: 4 -> 2; matrix products, arithmetic and copies ran while one was open for 0% -> 0% of each run, Pallas kernels for 0% -> 9%
where the time goes in v2:
time: 66.6 us; the launch traced here: 66.3 us
  blocking collectives  30.5 us (46%)
  Pallas kernels  20.3 us (30%)
  local copies, waits for them, and re-layouts  11.7 us (18%)
  waiting for transfers between devices  2.16 us (3%)
  starting transfers between devices  0.94 us (1%)
  between operations  0.69 us (1%)
    all_to_all x1, blocking collectives, by_columns(): lax.all_to_all(packed, AXES, 0, 0, axis_index_groups=groups, tiled=True)  17 us
    all_to_all x1, blocking collectives, by_columns(): lax.all_to_all(mixed, AXES, 0, 0, axis_index_groups=groups, tiled=True)  13.6 us
    unnamed x12, local copies, waits for them, and re-layouts  11.7 us
    pallas_call x1, Pallas kernels, by_columns(): call(second_kernel, [shape(cols, total), shape(cols, half), shape(cols, h...  6.44 us
    pallas_call x1, Pallas kernels, by_columns(): call(functools.partial(first_kernel, soft), [shape(PANEL, sizes[0], dtype...  5.97 us
    pallas_call x1, Pallas kernels, by_columns(): call(functools.partial(middle_kernel, soft), [shape(PANEL, sizes[1], dtyp...  5.17 us
    pallas_call x1, Pallas kernels, by_columns(): call(functools.partial(pack_kernel, 1.0 / kernel_scale, parts), [shape(pa...  1.71 us
  transfers between devices with their start and end apart: 3, of which 2 were waited for; matrix products, arithmetic and copies ran while one was open for 0% of the time, Pallas kernels for 9%

profile of v2, /device:TPU:0, one launch (start us, length us, event | category | flops | bytes accessed | tf_op | source)
XLA Modules:
  0.0 66.3 jit_solution(7129967350810000737)
XLA Ops:
  0.6 1.7 %shard_map.50 = f32[16,24,128]{2,1,0:T(8,128)} custom-call(f32[3,128]{1,0:T(4,128)} %pos_hbm.1, f32[1,128]{1,0:T(1,128)} %bitcast.2, f32[128,256]{1,0:T(8,128)} %rhs_hbm.1), custom_call_target="tpu_custom_call" | custom-call | tf_op jit(solution)/shard_map/pallas_call | solution.py:336
  2.3 17.0 %all_to_all.10.own_ref = f32[16,24,128]{2,1,0:T(8,128)S(1)} all-to-all(f32[16,24,128]{2,1,0:T(8,128)} %shard_map.50), channel_id=1, replica_groups={{0,2,4,6,8,10,12,14,16,18,20,22,24,26,28,30},{1,3,5,7,9,11,13,15,17,19,..., dimensions={0} | all-to-all | bytes 393216 | tf_op jit(solution)/shard_map/all_to_all | solution.py:348
  19.3 0.0 collective-permute-start
  19.3 6.0 %shard_map.51 = (bf16[256,9216]{1,0:T(8,128)(2,1)S(1)}, bf16[256,9216]{1,0:T(8,128)(2,1)S(1)}, bf16[7168,256]{1,0:T(8,128)(2,1)S(1)}, bf16[7168,256]{1,0:T(8,128...) custom-call(f32[16,24,128]{2,1,0:T(8,128)S(1)} %all_to_all.10.own_ref), custom_call_target="tpu_custom_call" | custom-call | tf_op jit(solution)/shard_map/pallas_call | solution.py:351
  25.3 0.0 collective-permute-done.oth_ref
  25.3 5.2 %shard_map.52 = (bf16[256,7168]{1,0:T(8,128)(2,1)S(1)}, bf16[256,7168]{1,0:T(8,128)(2,1)S(1)}, bf16[7168,256]{1,0:T(8,128)(2,1)S(1)}, bf16[7168,256]{1,0:T(8,128...) custom-call(s32[1]{0:T(128)} %bitcast.1.core_ref, f32[16,24,128]{2,1,0:T(8,128)S(1)} %all_to_all.10.own_ref, ...), custom_call_target="tpu_custom_call" | custom-call | tf_op jit(solution)/shard_map/pallas_call | solution.py:360
  30.5 0.0 copy-start
  30.5 1.8 %copy-done = bf16[256,7168]{1,0:T(8,128)(2,1)} copy-done((bf16[256,7168]{1,0:T(8,128)(2,1)}, bf16[256,7168]{1,0:T(8,128)(2,1)S(1)}, u32[]{:S(2)}) %copy-start) | copy-done | bytes 3670040
  32.3 0.0 copy-start.2
  32.3 1.8 %copy-done.2 = bf16[7168,256]{1,0:T(8,128)(2,1)} copy-done((bf16[7168,256]{1,0:T(8,128)(2,1)}, bf16[7168,256]{1,0:T(8,128)(2,1)S(1)}, u32[]{:S(2)}) %copy-start.2) | copy-done | bytes 3670040
  34.1 0.0 copy-start.4
  34.1 1.9 %copy-done.4 = bf16[7168,256]{1,0:T(8,128)(2,1)} copy-done((bf16[7168,256]{1,0:T(8,128)(2,1)}, bf16[7168,256]{1,0:T(8,128)(2,1)S(1)}, u32[]{:S(2)}) %copy-start.4) | copy-done | bytes 3670040
  36.0 0.5 collective-permute-start.1
  36.5 1.2 %collective-permute-done.1.theirs_ref = f32[16,4096]{1,0:T(8,128)S(1)} collective-permute-done((f32[16,4096]{1,0:T(8,128)S(1)}, f32[16,4096]{1,0:T(8,128)S(1)}, u32[]{:S(2)}, u32[]{:S(2)}) %collective-permute-start.1) | collective-permute-done | bytes 262176 | tf_op jit(solution)/shard_map/ppermute | solution.py:382
  37.7 0.0 copy-start.1
  37.7 2.0 %copy-done.1 = bf16[256,7168]{1,0:T(8,128)(2,1)S(1)} copy-done((bf16[256,7168]{1,0:T(8,128)(2,1)S(1)}, bf16[256,7168]{1,0:T(8,128)(2,1)}, u32[]{:S(2)}) %copy-start.1) | copy-done | bytes 3670040
  39.7 0.0 copy-start.3
  39.7 2.0 %copy-done.3 = bf16[7168,256]{1,0:T(8,128)(2,1)S(1)} copy-done((bf16[7168,256]{1,0:T(8,128)(2,1)S(1)}, bf16[7168,256]{1,0:T(8,128)(2,1)}, u32[]{:S(2)}) %copy-start.3) | copy-done | bytes 3670040
  41.8 0.0 copy-start.5
  41.8 2.0 %copy-done.5 = bf16[7168,256]{1,0:T(8,128)(2,1)S(1)} copy-done((bf16[7168,256]{1,0:T(8,128)(2,1)S(1)}, bf16[7168,256]{1,0:T(8,128)(2,1)}, u32[]{:S(2)}) %copy-start.5) | copy-done | bytes 3670040
  43.8 6.4 %shard_map.53 = (f32[16,4096]{1,0:T(8,128)S(1)}, f32[16,2048]{1,0:T(8,128)S(1)}, f32[16,2048]{1,0:T(8,128)S(1)}, f32[16,2176]{1,0:T(8,128)S(1)}, f32[2,16,128]{2,1,0:T(8,128)S(1)}) custom-call(s32[1]{0:T(128)} %bitcast.1.core_ref, f32[16,24,128]{2,1,0:T(8,128)S(1)} %all_to_all.10.own_ref, f32[16,24,128]{2,1,0:T(8,128)S(1)} %collective-permute-done.oth_ref, ...), custom_call_target="tpu_custom_call" | custom-call | tf_op jit(solution)/shard_map/pallas_call | solution.py:373
  50.3 0.4 collective-permute-start.2
  50.7 1.0 %collective-permute-done.2.come_ref = f32[16,2176]{1,0:T(8,128)S(1)} collective-permute-done((f32[16,2176]{1,0:T(8,128)S(1)}, f32[16,2176]{1,0:T(8,128)S(1)}, u32[]{:S(2)}, u32[]{:S(2)}) %collective-permute-start.2) | collective-permute-done | bytes 139296 | tf_op jit(solution)/shard_map/ppermute | solution.py:383
  51.7 0.2 shard_map.54
  51.9 13.6 %all_to_all.11.in_ref = f32[16,32,128]{2,1,0:T(8,128)S(1)} all-to-all(f32[16,32,128]{2,1,0:T(8,128)S(1)} %shard_map.54), channel_id=1, replica_groups={{0,2,4,6,8,10,12,14,16,18,20,22,24,26,28,30},{1,3,5,7,9,11,13,15,17,19,..., dimensions={0} | all-to-all | bytes 524288 | tf_op jit(solution)/shard_map/all_to_all | solution.py:387
  65.5 0.8 %shard_map.55 = (f32[128,256]{1,0:T(8,128)}, f32[128,256]{1,0:T(8,128)}) custom-call(f32[16,32,128]{2,1,0:T(8,128)S(1)} %all_to_all.11.in_ref), custom_call_target="tpu_custom_call" | custom-call | tf_op jit(solution)/shard_map/pallas_call | solution.py:388
Async XLA Ops:
  19.3 6.0 %collective-permute-start = (f32[16,24,128]{2,1,0:T(8,128)S(1)}, f32[16,24,128]{2,1,0:T(8,128)S(1)}, u32[]{:S(2)}, u32[]{:S(2)}) collective-permute-start(f32[16,24,128]{2,1,0:T(8,128)S(1)} %all_to_all.10.own_ref), channel_id=1, source_target_pairs={{0,1},{1,0},{2,3},{3,2},{4,5},{5,4},{6,7},{7,6},{8,9},{9,8},{10,11... | collective-permute-start | bytes 589832 | tf_op jit(solution)/shard_map/ppermute | solution.py:349
  30.5 1.8 %copy-start = (bf16[256,7168]{1,0:T(8,128)(2,1)}, bf16[256,7168]{1,0:T(8,128)(2,1)S(1)}, u32[]{:S(2)}) copy-start(bf16[256,7168]{1,0:T(8,128)(2,1)S(1)} %get-tuple-element.29.refs_5_) | copy-start | bytes 11010052
  32.3 1.8 %copy-start.2 = (bf16[7168,256]{1,0:T(8,128)(2,1)}, bf16[7168,256]{1,0:T(8,128)(2,1)S(1)}, u32[]{:S(2)}) copy-start(bf16[7168,256]{1,0:T(8,128)(2,1)S(1)} %get-tuple-element.30.refs_6_) | copy-start | bytes 11010052
  34.1 1.9 %copy-start.4 = (bf16[7168,256]{1,0:T(8,128)(2,1)}, bf16[7168,256]{1,0:T(8,128)(2,1)S(1)}, u32[]{:S(2)}) copy-start(bf16[7168,256]{1,0:T(8,128)(2,1)S(1)} %get-tuple-element.31.refs_7_) | copy-start | bytes 11010052
  36.0 1.7 %collective-permute-start.1 = (f32[16,4096]{1,0:T(8,128)S(1)}, f32[16,4096]{1,0:T(8,128)S(1)}, u32[]{:S(2)}, u32[]{:S(2)}) collective-permute-start(f32[16,4096]{1,0:T(8,128)S(1)} %get-tuple-element.23.mine_ref), channel_id=1, source_target_pairs={{0,1},{1,0},{2,3},{3,2},{4,5},{5,4},{6,7},{7,6},{8,9},{9,8},{10,11... | collective-permute-start | bytes 786440 | tf_op jit(solution)/shard_map/ppermute | solution.py:382
  37.7 2.0 %copy-start.1 = (bf16[256,7168]{1,0:T(8,128)(2,1)S(1)}, bf16[256,7168]{1,0:T(8,128)(2,1)}, u32[]{:S(2)}) copy-start(bf16[256,7168]{1,0:T(8,128)(2,1)} %copy-done) | copy-start | bytes 11010052
  39.7 2.0 %copy-start.3 = (bf16[7168,256]{1,0:T(8,128)(2,1)S(1)}, bf16[7168,256]{1,0:T(8,128)(2,1)}, u32[]{:S(2)}) copy-start(bf16[7168,256]{1,0:T(8,128)(2,1)} %copy-done.2) | copy-start | bytes 11010052
  41.8 2.0 %copy-start.5 = (bf16[7168,256]{1,0:T(8,128)(2,1)S(1)}, bf16[7168,256]{1,0:T(8,128)(2,1)}, u32[]{:S(2)}) copy-start(bf16[7168,256]{1,0:T(8,128)(2,1)} %copy-done.4) | copy-start | bytes 11010052
  50.3 1.4 %collective-permute-start.2 = (f32[16,2176]{1,0:T(8,128)S(1)}, f32[16,2176]{1,0:T(8,128)S(1)}, u32[]{:S(2)}, u32[]{:S(2)}) collective-permute-start(f32[16,2176]{1,0:T(8,128)S(1)} %get-tuple-element.36.send_ref), channel_id=1, source_target_pairs={{0,1},{1,0},{2,3},{3,2},{4,5},{5,4},{6,7},{7,6},{8,9},{9,8},{10,11... | collective-permute-start | bytes 417800 | tf_op jit(solution)/shard_map/ppermute | solution.py:383

commit v3 on v2

--- a/solution.py
+++ b/solution.py
@@ -368,7 +368,7 @@
             pltpu.VMEM((EXTRA, half), F32),
             pltpu.VMEM((2 * cols, half), BF16),
         ],
-        16,
+        8,
     )(core, own, oth, vec, sub, acc)
     direction, residual, image, send, stats = call(
         second_kernel,

time: 66.6 us -> 54.9 us (0.82)
  local copies, waits for them, and re-layouts: 11.7 us -> 0 us
    unnamed x12 -> x0, local copies, waits for them, and re-layouts: 11.7 us -> none
  transfers between devices with their start and end apart: 3 -> 3, of which waited for: 2 -> 2; matrix products, arithmetic and copies ran while one was open for 0% -> 0% of each run, Pallas kernels for 9% -> 11%
where the time goes in v3:
time: 54.9 us; the launch traced here: 54.6 us
  blocking collectives  30.5 us (56%)
  Pallas kernels  20.2 us (37%)
  waiting for transfers between devices  2.16 us (4%)
  starting transfers between devices  1.01 us (2%)
  between operations  0.67 us (1%)
    all_to_all x1, blocking collectives, by_columns(): lax.all_to_all(packed, AXES, 0, 0, axis_index_groups=groups, tiled=True)  17 us
    all_to_all x1, blocking collectives, by_columns(): lax.all_to_all(mixed, AXES, 0, 0, axis_index_groups=groups, tiled=True)  13.6 us
    pallas_call x1, Pallas kernels, by_columns(): call(second_kernel, [shape(cols, total), shape(cols, half), shape(cols, h...  6.38 us
    pallas_call x1, Pallas kernels, by_columns(): call(functools.partial(first_kernel, soft), [shape(PANEL, sizes[0], dtype...  5.97 us
    pallas_call x1, Pallas kernels, by_columns(): call(functools.partial(middle_kernel, soft), [shape(PANEL, sizes[1], dtyp...  5.18 us
    pallas_call x1, Pallas kernels, by_columns(): call(functools.partial(pack_kernel, 1.0 / kernel_scale, parts), [shape(pa...  1.7 us
    ppermute x1, waiting for transfers between devices, by_columns(): lax.ppermute(mine, 'col', swap)  1.16 us
  transfers between devices with their start and end apart: 3, of which 2 were waited for; matrix products, arithmetic and copies ran while one was open for 0% of the time, Pallas kernels for 11%

profile of v3, /device:TPU:0, one launch (start us, length us, event | category | flops | bytes accessed | tf_op | source)
XLA Modules:
  0.0 54.6 jit_solution(1937776855639046863)
XLA Ops:
  0.6 1.7 %shard_map.50 = f32[16,24,128]{2,1,0:T(8,128)} custom-call(f32[3,128]{1,0:T(4,128)} %pos_hbm.1, f32[1,128]{1,0:T(1,128)} %bitcast.2, f32[128,256]{1,0:T(8,128)} %rhs_hbm.1), custom_call_target="tpu_custom_call" | custom-call | tf_op jit(solution)/shard_map/pallas_call | solution.py:336
  2.3 17.0 %all_to_all.10.own_ref = f32[16,24,128]{2,1,0:T(8,128)S(1)} all-to-all(f32[16,24,128]{2,1,0:T(8,128)} %shard_map.50), channel_id=1, replica_groups={{0,2,4,6,8,10,12,14,16,18,20,22,24,26,28,30},{1,3,5,7,9,11,13,15,17,19,..., dimensions={0} | all-to-all | bytes 393216 | tf_op jit(solution)/shard_map/all_to_all | solution.py:348
  19.3 0.0 collective-permute-start
  19.3 6.0 %shard_map.51 = (bf16[256,9216]{1,0:T(8,128)(2,1)S(1)}, bf16[256,9216]{1,0:T(8,128)(2,1)S(1)}, bf16[7168,256]{1,0:T(8,128)(2,1)S(1)}, bf16[7168,256]{1,0:T(8,128...) custom-call(f32[16,24,128]{2,1,0:T(8,128)S(1)} %all_to_all.10.own_ref), custom_call_target="tpu_custom_call" | custom-call | tf_op jit(solution)/shard_map/pallas_call | solution.py:351
  25.3 0.0 collective-permute-done.oth_ref
  25.3 5.2 %shard_map.52 = (bf16[256,7168]{1,0:T(8,128)(2,1)S(1)}, bf16[256,7168]{1,0:T(8,128)(2,1)S(1)}, bf16[7168,256]{1,0:T(8,128)(2,1)S(1)}, bf16[7168,256]{1,0:T(8,128...) custom-call(s32[1]{0:T(128)} %bitcast.1.core_ref, f32[16,24,128]{2,1,0:T(8,128)S(1)} %all_to_all.10.own_ref, ...), custom_call_target="tpu_custom_call" | custom-call | tf_op jit(solution)/shard_map/pallas_call | solution.py:360
  30.5 0.6 %collective-permute-start.1 = (f32[16,4096]{1,0:T(8,128)S(1)}, f32[16,4096]{1,0:T(8,128)S(1)}, u32[]{:S(2)}, u32[]{:S(2)}) collective-permute-start(f32[16,4096]{1,0:T(8,128)S(1)} %get-tuple-element.23.mine_ref), channel_id=1, source_target_pairs={{0,1},{1,0},{2,3},{3,2},{4,5},{5,4},{6,7},{7,6},{8,9},{9,8},{10,11... | collective-permute-start | bytes 786440 | tf_op jit(solution)/shard_map/ppermute | solution.py:382
  31.0 1.2 %collective-permute-done.1.theirs_ref = f32[16,4096]{1,0:T(8,128)S(1)} collective-permute-done((f32[16,4096]{1,0:T(8,128)S(1)}, f32[16,4096]{1,0:T(8,128)S(1)}, u32[]{:S(2)}, u32[]{:S(2)}) %collective-permute-start.1) | collective-permute-done | bytes 262176 | tf_op jit(solution)/shard_map/ppermute | solution.py:382
  32.2 6.4 %shard_map.53 = (f32[16,4096]{1,0:T(8,128)S(1)}, f32[16,2048]{1,0:T(8,128)S(1)}, f32[16,2048]{1,0:T(8,128)S(1)}, f32[16,2176]{1,0:T(8,128)S(1)}, f32[2,16,128]{2,1,0:T(8,128)S(1)}) custom-call(s32[1]{0:T(128)} %bitcast.1.core_ref, f32[16,24,128]{2,1,0:T(8,128)S(1)} %all_to_all.10.own_ref, f32[16,24,128]{2,1,0:T(8,128)S(1)} %collective-permute-done.oth_ref, ...), custom_call_target="tpu_custom_call" | custom-call | tf_op jit(solution)/shard_map/pallas_call | solution.py:373
  38.6 0.4 collective-permute-start.2
  39.0 1.0 %collective-permute-done.2.come_ref = f32[16,2176]{1,0:T(8,128)S(1)} collective-permute-done((f32[16,2176]{1,0:T(8,128)S(1)}, f32[16,2176]{1,0:T(8,128)S(1)}, u32[]{:S(2)}, u32[]{:S(2)}) %collective-permute-start.2) | collective-permute-done | bytes 139296 | tf_op jit(solution)/shard_map/ppermute | solution.py:383
  40.0 0.2 shard_map.54
  40.2 13.6 %all_to_all.11.in_ref = f32[16,32,128]{2,1,0:T(8,128)S(1)} all-to-all(f32[16,32,128]{2,1,0:T(8,128)S(1)} %shard_map.54), channel_id=1, replica_groups={{0,2,4,6,8,10,12,14,16,18,20,22,24,26,28,30},{1,3,5,7,9,11,13,15,17,19,..., dimensions={0} | all-to-all | bytes 524288 | tf_op jit(solution)/shard_map/all_to_all | solution.py:387
  53.8 0.8 %shard_map.55 = (f32[128,256]{1,0:T(8,128)}, f32[128,256]{1,0:T(8,128)}) custom-call(f32[16,32,128]{2,1,0:T(8,128)S(1)} %all_to_all.11.in_ref), custom_call_target="tpu_custom_call" | custom-call | tf_op jit(solution)/shard_map/pallas_call | solution.py:388
Async XLA Ops:
  19.3 6.0 %collective-permute-start = (f32[16,24,128]{2,1,0:T(8,128)S(1)}, f32[16,24,128]{2,1,0:T(8,128)S(1)}, u32[]{:S(2)}, u32[]{:S(2)}) collective-permute-start(f32[16,24,128]{2,1,0:T(8,128)S(1)} %all_to_all.10.own_ref), channel_id=1, source_target_pairs={{0,1},{1,0},{2,3},{3,2},{4,5},{5,4},{6,7},{7,6},{8,9},{9,8},{10,11... | collective-permute-start | bytes 589832 | tf_op jit(solution)/shard_map/ppermute | solution.py:349
  30.5 1.7 %collective-permute-start.1 = (f32[16,4096]{1,0:T(8,128)S(1)}, f32[16,4096]{1,0:T(8,128)S(1)}, u32[]{:S(2)}, u32[]{:S(2)}) collective-permute-start(f32[16,4096]{1,0:T(8,128)S(1)} %get-tuple-element.23.mine_ref), channel_id=1, source_target_pairs={{0,1},{1,0},{2,3},{3,2},{4,5},{5,4},{6,7},{7,6},{8,9},{9,8},{10,11... | collective-permute-start | bytes 786440 | tf_op jit(solution)/shard_map/ppermute | solution.py:382
  38.6 1.4 %collective-permute-start.2 = (f32[16,2176]{1,0:T(8,128)S(1)}, f32[16,2176]{1,0:T(8,128)S(1)}, u32[]{:S(2)}, u32[]{:S(2)}) collective-permute-start(f32[16,2176]{1,0:T(8,128)S(1)} %get-tuple-element.36.send_ref), channel_id=1, source_target_pairs={{0,1},{1,0},{2,3},{3,2},{4,5},{5,4},{6,7},{7,6},{8,9},{9,8},{10,11... | collective-permute-start | bytes 417800 | tf_op jit(solution)/shard_map/ppermute | solution.py:383

commit v4 on v3

--- a/solution.py
+++ b/solution.py
@@ -108,7 +108,9 @@
 
 
 def product(vec, high, low):
-    return jnp.dot(vec, high, preferred_element_type=F32) + jnp.dot(vec, low, preferred_element_type=F32)
+    cols = vec.shape[0] // 2
+    both = jnp.dot(vec, high, preferred_element_type=F32)
+    return both[0:cols] + both[cols:] + jnp.dot(vec[0:cols], low, preferred_element_type=F32)
 
 
 def evaluate(soft, sub_ref, rows, lane_ref, at):
@@ -212,8 +214,8 @@
     for q in range(parts):
         at = slice(q * LANES, (q + 1) * LANES)
         here = own_ref[q, 0:cols, :] / own_ref[q, cols + 3 : cols + 4, :]
-        image_ref[:, at] = acc_ref[0:cols, at] + acc_ref[cols : 2 * cols, at] + here
-    image_ref[:, half:] = acc_ref[0:cols, half:] + acc_ref[cols : 2 * cols, half:]
+        image_ref[:, at] = acc_ref[:, at] + here
+    image_ref[:, half:] = acc_ref[:, half:]
 
 
 def second_kernel(core_ref, own_ref, oth_ref, mine_ref, theirs_ref, *refs):
@@ -273,7 +275,7 @@
     curve = zero
     for n, (ref, q, at) in enumerate(blocks):
         direction = dir_ref[:, at]
-        image = acc_ref[0:cols, at] + acc_ref[cols : 2 * cols, at]
+        image = acc_ref[:, at]
         if n < parts:
             image = image + direction / own_ref[q, cols + 3 : cols + 4, :]
             image_ref[:, at] = image
@@ -343,8 +345,7 @@
             pltpu.VMEM((LANES, columns), F32),
             pltpu.SemaphoreType.DMA((3,)),
         ],
-        60,
-    )(positions, radii.reshape(1, -1), right_side)
+    )(*[pltpu.with_memory_space_constraint(x, pltpu.HBM) for x in (positions, radii.reshape(1, -1), right_side)])
     own = lax.all_to_all(packed, AXES, 0, 0, axis_index_groups=groups, tiled=True)
     oth = lax.ppermute(own, "col", swap)
     sizes = [sum(cs.stop - cs.start for _, cs, _ in spans(panels)) for spans in (near_spans, across_spans)]
@@ -352,7 +353,7 @@
         functools.partial(first_kernel, soft),
         [shape(PANEL, sizes[0], dtype=BF16)] * 2
         + [shape(sizes[0] - half, PANEL, dtype=BF16)] * 2
-        + [shape(2 * cols, half, dtype=BF16), shape(3, half, LANES), shape(2 * cols, half)],
+        + [shape(2 * cols, half, dtype=BF16), shape(3, half, LANES), shape(cols, half)],
         [VM],
         [pltpu.VMEM((EXTRA, half), F32)],
         16,
@@ -364,7 +365,7 @@
         + [shape(panels // 2, 4, PANEL, PANEL, dtype=BF16), shape(cols, total)],
         [SM] + [VM] * 5,
         [
-            pltpu.VMEM((2 * cols, total), F32),
+            pltpu.VMEM((cols, total), F32),
             pltpu.VMEM((EXTRA, half), F32),
             pltpu.VMEM((2 * cols, half), BF16),
         ],
@@ -376,7 +377,7 @@
         [SM] + [VM] * 13,
         [
             pltpu.VMEM((2 * cols, total), BF16),
-            pltpu.VMEM((2 * cols, total), F32),
+            pltpu.VMEM((cols, total), F32),
             pltpu.VMEM((cols, total), F32),
         ],
     )(core, own, oth, mine, lax.ppermute(mine, "col", swap), *near, *across)

time: 54.9 us -> 52.3 us (0.953)
  Pallas kernels: 20.2 us -> 18 us
    pallas_call x1, Pallas kernels: 6.38 us -> 5.29 us  [by_columns(): call(second_kernel, [shape(cols, total), shape(cols, half), shape(cols, h...]
    pallas_call x1, Pallas kernels: 1.7 us -> 1.03 us  [by_columns(): call(functools.partial(pack_kernel, 1.0 / kernel_scale, parts), [shape(pa...]
where the time goes in v4:
time: 52.3 us; the launch traced here: 52.1 us
  blocking collectives  30.3 us (58%)
  Pallas kernels  18 us (34%)
  waiting for transfers between devices  2.16 us (4%)
  starting transfers between devices  1.01 us (2%)
  between operations  0.67 us (1%)
    all_to_all x1, blocking collectives, by_columns(): lax.all_to_all(packed, AXES, 0, 0, axis_index_groups=groups, tiled=True)  16.8 us
    all_to_all x1, blocking collectives, by_columns(): lax.all_to_all(mixed, AXES, 0, 0, axis_index_groups=groups, tiled=True)  13.6 us
    pallas_call x1, Pallas kernels, by_columns(): call(functools.partial(first_kernel, soft), [shape(PANEL, sizes[0], dtype...  5.77 us
    pallas_call x1, Pallas kernels, by_columns(): call(second_kernel, [shape(cols, total), shape(cols, half), shape(cols, h...  5.29 us
    pallas_call x1, Pallas kernels, by_columns(): call(functools.partial(middle_kernel, soft), [shape(PANEL, sizes[1], dtyp...  4.88 us
    ppermute x1, waiting for transfers between devices, by_columns(): lax.ppermute(mine, 'col', swap)  1.16 us
  transfers between devices with their start and end apart: 3, of which 2 were waited for; matrix products, arithmetic and copies ran while one was open for 0% of the time, Pallas kernels for 11%

profile of v4, /device:TPU:0, one launch (start us, length us, event | category | flops | bytes accessed | tf_op | source)
XLA Modules:
  0.0 52.1 jit_solution(3423953313698451787)
XLA Ops:
  0.6 1.0 %shard_map.50 = f32[16,24,128]{2,1,0:T(8,128)S(1)} custom-call(f32[3,128]{1,0:T(4,128)} %pos_hbm.1, f32[1,128]{1,0:T(1,128)} %bitcast.2, f32[128,256]{1,0:T(8,128)} %rhs_hbm.1), custom_call_target="tpu_custom_call" | custom-call | tf_op jit(solution)/shard_map/pallas_call | solution.py:338
  1.7 16.8 %all_to_all.10.own_ref = f32[16,24,128]{2,1,0:T(8,128)S(1)} all-to-all(f32[16,24,128]{2,1,0:T(8,128)S(1)} %shard_map.50), channel_id=1, replica_groups={{0,2,4,6,8,10,12,14,16,18,20,22,24,26,28,30},{1,3,5,7,9,11,13,15,17,19,..., dimensions={0} | all-to-all | bytes 393216 | tf_op jit(solution)/shard_map/all_to_all | solution.py:349
  18.4 0.0 collective-permute-start
  18.4 5.8 %shard_map.51 = (bf16[256,9216]{1,0:T(8,128)(2,1)S(1)}, bf16[256,9216]{1,0:T(8,128)(2,1)S(1)}, bf16[7168,256]{1,0:T(8,128)(2,1)S(1)}, bf16[7168,256]{1,0:T(8,128...) custom-call(f32[16,24,128]{2,1,0:T(8,128)S(1)} %all_to_all.10.own_ref), custom_call_target="tpu_custom_call" | custom-call | tf_op jit(solution)/shard_map/pallas_call | solution.py:352
  24.2 0.0 collective-permute-done.oth_ref
  24.2 4.9 %shard_map.52 = (bf16[256,7168]{1,0:T(8,128)(2,1)S(1)}, bf16[256,7168]{1,0:T(8,128)(2,1)S(1)}, bf16[7168,256]{1,0:T(8,128)(2,1)S(1)}, bf16[7168,256]{1,0:T(8,128...) custom-call(s32[1]{0:T(128)} %bitcast.1.core_ref, f32[16,24,128]{2,1,0:T(8,128)S(1)} %all_to_all.10.own_ref, ...), custom_call_target="tpu_custom_call" | custom-call | tf_op jit(solution)/shard_map/pallas_call | solution.py:361
  29.1 0.6 %collective-permute-start.1 = (f32[16,4096]{1,0:T(8,128)S(1)}, f32[16,4096]{1,0:T(8,128)S(1)}, u32[]{:S(2)}, u32[]{:S(2)}) collective-permute-start(f32[16,4096]{1,0:T(8,128)S(1)} %get-tuple-element.23.mine_ref), channel_id=1, source_target_pairs={{0,1},{1,0},{2,3},{3,2},{4,5},{5,4},{6,7},{7,6},{8,9},{9,8},{10,11... | collective-permute-start | bytes 786440 | tf_op jit(solution)/shard_map/ppermute | solution.py:383
  29.7 1.2 %collective-permute-done.1.theirs_ref = f32[16,4096]{1,0:T(8,128)S(1)} collective-permute-done((f32[16,4096]{1,0:T(8,128)S(1)}, f32[16,4096]{1,0:T(8,128)S(1)}, u32[]{:S(2)}, u32[]{:S(2)}) %collective-permute-start.1) | collective-permute-done | bytes 262176 | tf_op jit(solution)/shard_map/ppermute | solution.py:383
  30.8 5.3 %shard_map.53 = (f32[16,4096]{1,0:T(8,128)S(1)}, f32[16,2048]{1,0:T(8,128)S(1)}, f32[16,2048]{1,0:T(8,128)S(1)}, f32[16,2176]{1,0:T(8,128)S(1)}, f32[2,16,128]{2,1,0:T(8,128)S(1)}) custom-call(s32[1]{0:T(128)} %bitcast.1.core_ref, f32[16,24,128]{2,1,0:T(8,128)S(1)} %all_to_all.10.own_ref, f32[16,24,128]{2,1,0:T(8,128)S(1)} %collective-permute-done.oth_ref, ...), custom_call_target="tpu_custom_call" | custom-call | tf_op jit(solution)/shard_map/pallas_call | solution.py:374
  36.1 0.4 collective-permute-start.2
  36.6 1.0 %collective-permute-done.2.come_ref = f32[16,2176]{1,0:T(8,128)S(1)} collective-permute-done((f32[16,2176]{1,0:T(8,128)S(1)}, f32[16,2176]{1,0:T(8,128)S(1)}, u32[]{:S(2)}, u32[]{:S(2)}) %collective-permute-start.2) | collective-permute-done | bytes 139296 | tf_op jit(solution)/shard_map/ppermute | solution.py:384
  37.6 0.2 shard_map.54
  37.8 13.6 %all_to_all.11.in_ref = f32[16,32,128]{2,1,0:T(8,128)S(1)} all-to-all(f32[16,32,128]{2,1,0:T(8,128)S(1)} %shard_map.54), channel_id=1, replica_groups={{0,2,4,6,8,10,12,14,16,18,20,22,24,26,28,30},{1,3,5,7,9,11,13,15,17,19,..., dimensions={0} | all-to-all | bytes 524288 | tf_op jit(solution)/shard_map/all_to_all | solution.py:388
  51.3 0.8 %shard_map.55 = (f32[128,256]{1,0:T(8,128)}, f32[128,256]{1,0:T(8,128)}) custom-call(f32[16,32,128]{2,1,0:T(8,128)S(1)} %all_to_all.11.in_ref), custom_call_target="tpu_custom_call" | custom-call | tf_op jit(solution)/shard_map/pallas_call | solution.py:389
Async XLA Ops:
  18.4 5.8 %collective-permute-start = (f32[16,24,128]{2,1,0:T(8,128)S(1)}, f32[16,24,128]{2,1,0:T(8,128)S(1)}, u32[]{:S(2)}, u32[]{:S(2)}) collective-permute-start(f32[16,24,128]{2,1,0:T(8,128)S(1)} %all_to_all.10.own_ref), channel_id=1, source_target_pairs={{0,1},{1,0},{2,3},{3,2},{4,5},{5,4},{6,7},{7,6},{8,9},{9,8},{10,11... | collective-permute-start | bytes 589832 | tf_op jit(solution)/shard_map/ppermute | solution.py:350
  29.1 1.7 %collective-permute-start.1 = (f32[16,4096]{1,0:T(8,128)S(1)}, f32[16,4096]{1,0:T(8,128)S(1)}, u32[]{:S(2)}, u32[]{:S(2)}) collective-permute-start(f32[16,4096]{1,0:T(8,128)S(1)} %get-tuple-element.23.mine_ref), channel_id=1, source_target_pairs={{0,1},{1,0},{2,3},{3,2},{4,5},{5,4},{6,7},{7,6},{8,9},{9,8},{10,11... | collective-permute-start | bytes 786440 | tf_op jit(solution)/shard_map/ppermute | solution.py:383
  36.1 1.4 %collective-permute-start.2 = (f32[16,2176]{1,0:T(8,128)S(1)}, f32[16,2176]{1,0:T(8,128)S(1)}, u32[]{:S(2)}, u32[]{:S(2)}) collective-permute-start(f32[16,2176]{1,0:T(8,128)S(1)} %get-tuple-element.36.send_ref), channel_id=1, source_target_pairs={{0,1},{1,0},{2,3},{3,2},{4,5},{5,4},{6,7},{7,6},{8,9},{9,8},{10,11... | collective-permute-start | bytes 417800 | tf_op jit(solution)/shard_map/ppermute | solution.py:384

commit v5 on v4

--- a/solution.py
+++ b/solution.py
@@ -14,7 +14,9 @@
 LANES = 128
 EXTRA = 8
 PANEL = 256
-WIDE = 512
+WIDE = 1024
+AHEAD = 2
+DEPTH = 48
 VM = pl.BlockSpec(memory_space=pltpu.VMEM)
 SM = pl.BlockSpec(memory_space=pltpu.SMEM)
 KERNEL_BYTES = 32 << 20
@@ -83,7 +85,7 @@
     return (solution, residual)
 
 
-def pack_kernel(scale, parts, pos_hbm, rad_hbm, rhs_hbm, out_ref, pos_ref, rad_ref, rhs_ref, sems):
+def pack_kernel(parts, pos_hbm, rad_hbm, rhs_hbm, out_ref, pos_ref, rad_ref, rhs_ref, sems):
     copies = [
         pltpu.make_async_copy(src, dst, sems.at[n])
         for n, (src, dst) in enumerate(((rhs_hbm, rhs_ref), (pos_hbm, pos_ref), (rad_hbm, rad_ref)))
@@ -95,7 +97,7 @@
     cols = rhs_ref.shape[1] // parts
     flipped = rhs_ref[...].T
     extra = jnp.concatenate(
-        [pos_ref[...] * scale, rad_ref[...], jnp.zeros((EXTRA - 4, LANES), F32)], axis=0
+        [pos_ref[...], rad_ref[...], jnp.zeros((EXTRA - 4, LANES), F32)], axis=0
     )
     for q in range(parts):
         out_ref[q, 0:cols, :] = flipped[q * cols : (q + 1) * cols, :]
@@ -113,32 +115,59 @@
     return both[0:cols] + both[cols:] + jnp.dot(vec[0:cols], low, preferred_element_type=F32)
 
 
-def evaluate(soft, sub_ref, rows, lane_ref, at):
-    starts = [sub_ref[c, rows, :] for c in range(3)]
-    ends = [lane_ref[c : c + 1, at] for c in range(3)]
-    high, low = [], []
-    for s in range(0, ends[0].shape[1], LANES):
-        gaps = [starts[c] - ends[c][:, s : s + LANES] for c in range(3)]
-        squared = gaps[0] * gaps[0] + gaps[1] * gaps[1] + gaps[2] * gaps[2]
-        a, b = split(lax.rsqrt(squared + soft))
-        high.append(a)
-        low.append(b)
-    return jnp.concatenate(high, 1), jnp.concatenate(low, 1)
-
-
-def unpack(ref, lane_ref, vec_ref, sub_ref=None):
+def evaluate(left_ref, right_ref, tasks):
+    begun = []
+    for n in range(len(tasks) + AHEAD):
+        if n < len(tasks):
+            rows, at, _ = tasks[n]
+            begun.append(jnp.dot(left_ref[rows, :], right_ref[:, at], preferred_element_type=F32))
+        if n >= AHEAD:
+            tasks[n - AHEAD][2](*split(lax.rsqrt(begun[n - AHEAD])))
+
+
+def pieces(values, count):
+    out = []
+    for _ in range(count):
+        part = values.astype(BF16).astype(F32)
+        values = values - part
+        out.append(part)
+    return out
+
+
+def factors(ref, soft, fact_ref, right_ref, left_ref=None):
+    parts, cols = ref.shape[0], ref.shape[1] - EXTRA
+    place = jnp.concatenate([ref[q, cols : cols + 3, :] for q in range(parts)], axis=1) * 512.0 - 256.0
+    whole = jnp.floor(place + 0.5)
+    rest, more = pieces(place - whole, 2)
+    both = rest + more
+    one = jnp.ones_like(place[0:1])
+    norm = pieces(jnp.sum(whole * whole, axis=0, keepdims=True), 3)
+    cross = jnp.sum((2.0 * whole + both) * both, axis=0, keepdims=True)
+
+    def write(rows):
+        at = 0
+        for row in rows:
+            fact_ref[at : at + row.shape[0], :] = row
+            at += row.shape[0]
+
+    fact_ref[...] = jnp.zeros_like(fact_ref)
+    twice, less, least = -2.0 * whole, -2.0 * rest, -2.0 * more
+    write([twice, one, one, one, *norm, one, one, one, *pieces(cross + soft, 3), less, least, twice, twice, less, least, less])
+    right_ref[...] = fact_ref[0 : right_ref.shape[0], :].astype(BF16)
+    if left_ref is not None:
+        write([whole, *norm, one, one, one, *pieces(cross, 3), one, one, one, whole, whole, rest, more, rest, rest, more])
+        for q in range(parts):
+            at = slice(q * LANES, (q + 1) * LANES)
+            left_ref[at, :] = fact_ref[:, at].T[:, 0 : left_ref.shape[1]].astype(BF16)
+
+
+def unpack(factor, ref, vec_ref):
     parts, cols = ref.shape[0], ref.shape[1] - EXTRA
     for q in range(parts):
         at = slice(q * LANES, (q + 1) * LANES)
-        high, low = split(ref[q, 0:cols, :])
+        high, low = split(ref[q, 0:cols, :] * factor)
         vec_ref[0:cols, at] = high
         vec_ref[cols : 2 * cols, at] = low
-        extra = ref[q, cols : cols + EXTRA, :]
-        lane_ref[:, at] = extra
-        if sub_ref is not None:
-            turned = extra.T
-            for c in range(3):
-                sub_ref[c, at, :] = jnp.broadcast_to(turned[:, c : c + 1], (LANES, LANES))
 
 
 def near_spans(panels):
@@ -157,60 +186,73 @@
     return spans
 
 
-def first_kernel(soft, own_ref, high_ref, low_ref, high_t_ref, low_t_ref, vec_ref, sub_ref, acc_ref, lane_ref):
+def first_kernel(soft, factor, own_ref, high_ref, low_ref, high_t_ref, low_t_ref, vec_ref, left_ref, acc_ref, right_ref, fact_ref):
     panels = vec_ref.shape[1] // PANEL
-    unpack(own_ref, lane_ref, vec_ref, sub_ref)
+    unpack(factor, own_ref, vec_ref)
+    factors(own_ref, soft, fact_ref, right_ref, left_ref)
     acc_ref[...] = jnp.zeros_like(acc_ref)
+    tasks = []
     for t, columns, start in near_spans(panels):
         rows = slice(t * PANEL, (t + 1) * PANEL)
         for c in range(columns.start, columns.stop, WIDE):
             at = slice(c, min(c + WIDE, columns.stop))
-            high, low = evaluate(soft, sub_ref, rows, lane_ref, at)
-            to = start + c - columns.start
-            high_ref[:, to : to + at.stop - c] = high
-            low_ref[:, to : to + at.stop - c] = low
-            acc_ref[:, at] += product(vec_ref[:, rows], high, low)
-            skip = PANEL if c == columns.start else 0
-            if at.stop - c > skip:
-                high, low = high[:, skip:].T, low[:, skip:].T
-                to = to + skip - (t + 1) * PANEL
-                high_t_ref[to : to + at.stop - c - skip, :] = high
-                low_t_ref[to : to + at.stop - c - skip, :] = low
-                acc_ref[:, rows] += product(vec_ref[:, c + skip : at.stop], high, low)
-
-
-def middle_kernel(soft, core_ref, own_ref, oth_ref, vec_ref, sub_ref, near_ref, *refs):
-    high_ref, low_ref, high_t_ref, low_t_ref, far_ref, image_ref, acc_ref, lane_ref, vec_oth_ref = refs
+
+            def use(high, low, t=t, rows=rows, at=at, to=start + c - columns.start, skip=PANEL if c == columns.start else 0):
+                wide = at.stop - at.start
+                high_ref[:, to : to + wide] = high
+                low_ref[:, to : to + wide] = low
+                acc_ref[:, at] += product(vec_ref[:, rows], high, low)
+                if wide > skip:
+                    high, low = high[:, skip:].T, low[:, skip:].T
+                    to = to + skip - (t + 1) * PANEL
+                    high_t_ref[to : to + wide - skip, :] = high
+                    low_t_ref[to : to + wide - skip, :] = low
+                    acc_ref[:, rows] += product(vec_ref[:, at.start + skip : at.stop], high, low)
+
+            tasks.append((rows, at, use))
+    evaluate(left_ref, right_ref, tasks)
+
+
+def middle_kernel(soft, factor, core_ref, own_ref, oth_ref, vec_ref, left_ref, near_ref, *refs):
+    high_ref, low_ref, high_t_ref, low_t_ref, far_ref, image_ref, acc_ref, right_ref, vec_oth_ref, fact_ref = refs
     parts, cols = own_ref.shape[0], own_ref.shape[1] - EXTRA
     half = parts * LANES
     panels = half // PANEL
-    unpack(oth_ref, lane_ref, vec_oth_ref)
+    unpack(factor, oth_ref, vec_oth_ref)
+    factors(oth_ref, soft, fact_ref, right_ref)
     acc_ref[:, 0:half] = near_ref[...]
     acc_ref[:, half:] = jnp.zeros_like(near_ref)
+    tasks = []
+    for n in range(panels // 2):
+        place = pl.multiple_of((core_ref[0] * (panels // 2) + n) * PANEL, PANEL)
+        rows, there = pl.ds(place, PANEL), pl.ds(pl.multiple_of(half + place, PANEL), PANEL)
+
+        def use_far(high, low, n=n, rows=rows, there=there):
+            far_ref[n, 0] = high
+            far_ref[n, 1] = low
+            acc_ref[:, there] += product(vec_ref[:, rows], high, low)
+            high, low = high.T, low.T
+            far_ref[n, 2] = high
+            far_ref[n, 3] = low
+            acc_ref[:, rows] += product(vec_oth_ref[:, rows], high, low)
+
+        tasks.append((rows, rows, use_far))
     for t, columns, start in across_spans(panels):
         rows = slice(t * PANEL, (t + 1) * PANEL)
         for c in range(columns.start, columns.stop, WIDE):
             at = slice(c, min(c + WIDE, columns.stop))
-            high, low = evaluate(soft, sub_ref, rows, lane_ref, at)
-            to = slice(start + c, start + at.stop)
-            high_ref[:, to] = high
-            low_ref[:, to] = low
-            acc_ref[:, half + c : half + at.stop] += product(vec_ref[:, rows], high, low)
-            high, low = high.T, low.T
-            high_t_ref[to, :] = high
-            low_t_ref[to, :] = low
-            acc_ref[:, rows] += product(vec_oth_ref[:, at], high, low)
-    for n in range(panels // 2):
-        place = pl.multiple_of((core_ref[0] * (panels // 2) + n) * PANEL, PANEL)
-        rows, at = pl.ds(place, PANEL), pl.ds(pl.multiple_of(half + place, PANEL), PANEL)
-        high, low = evaluate(soft, sub_ref, rows, lane_ref, rows)
-        far_ref[n, 0] = high
-        far_ref[n, 1] = low
-        acc_ref[:, at] += product(vec_ref[:, rows], high, low)
-        high, low = high.T, low.T
-        far_ref[n, 2] = high
-        far_ref[n, 3] = low
-        acc_ref[:, rows] += product(vec_oth_ref[:, rows], high, low)
+
+            def use(high, low, rows=rows, at=at, to=slice(start + c, start + at.stop)):
+                high_ref[:, to] = high
+                low_ref[:, to] = low
+                acc_ref[:, half + at.start : half + at.stop] += product(vec_ref[:, rows], high, low)
+                high, low = high.T, low.T
+                high_t_ref[to, :] = high
+                low_t_ref[to, :] = low
+                acc_ref[:, rows] += product(vec_oth_ref[:, at], high, low)
+
+            tasks.append((rows, at, use))
+    evaluate(left_ref, right_ref, tasks)
     for q in range(parts):
         at = slice(q * LANES, (q + 1) * LANES)
         here = own_ref[q, 0:cols, :] / own_ref[q, cols + 3 : cols + 4, :]
@@ -218,7 +260,7 @@
     image_ref[:, half:] = acc_ref[:, half:]
 
 
-def second_kernel(core_ref, own_ref, oth_ref, mine_ref, theirs_ref, *refs):
+def second_kernel(factor, core_ref, own_ref, oth_ref, mine_ref, theirs_ref, *refs):
     near, across, far_ref = refs[0:4], refs[4:8], refs[8]
     dir_ref, res_ref, image_ref, send_ref, stat_ref, vec_ref, acc_ref, sum_ref = refs[9:]
     parts, cols = own_ref.shape[0], own_ref.shape[1] - EXTRA
@@ -251,7 +293,7 @@
         if n < parts:
             res_ref[:, at] = left
         dir_ref[:, at] = direction
-        high, low = split(direction)
+        high, low = split(direction * factor)
         vec_ref[0:cols, at] = high
         vec_ref[cols : 2 * cols, at] = low
     acc_ref[...] = jnp.zeros_like(acc_ref)
@@ -330,13 +372,13 @@
     half = total // 2
     panels = half // PANEL
     kernel_scale, softening = constants(total)
-    soft = softening / (kernel_scale * kernel_scale)
+    soft, factor = softening * 4.0**9, kernel_scale * 2.0**9
     groups = [[2 * chip + core for chip in range(parts)] for core in range(2)]
     swap = [(i, i ^ 1) for i in range(col_size)]
     core = (lax.axis_index("col") % 2).astype(jnp.int32).reshape(1)
 
     (packed,) = call(
-        functools.partial(pack_kernel, 1.0 / kernel_scale, parts),
+        functools.partial(pack_kernel, parts),
         [shape(parts, cols + EXTRA, LANES)],
         [pl.BlockSpec(memory_space=pltpu.HBM)] * 3,
         [
@@ -349,30 +391,31 @@
     own = lax.all_to_all(packed, AXES, 0, 0, axis_index_groups=groups, tiled=True)
     oth = lax.ppermute(own, "col", swap)
     sizes = [sum(cs.stop - cs.start for _, cs, _ in spans(panels)) for spans in (near_spans, across_spans)]
-    *near, vec, sub, acc = call(
-        functools.partial(first_kernel, soft),
+    *near, vec, left, acc = call(
+        functools.partial(first_kernel, soft, factor),
         [shape(PANEL, sizes[0], dtype=BF16)] * 2
         + [shape(sizes[0] - half, PANEL, dtype=BF16)] * 2
-        + [shape(2 * cols, half, dtype=BF16), shape(3, half, LANES), shape(cols, half)],
+        + [shape(2 * cols, half, dtype=BF16), shape(half, DEPTH, dtype=BF16), shape(cols, half)],
         [VM],
-        [pltpu.VMEM((EXTRA, half), F32)],
+        [pltpu.VMEM((DEPTH, half), BF16), pltpu.VMEM((LANES, half), F32)],
         16,
     )(own)
     *across, mine = call(
-        functools.partial(middle_kernel, soft),
+        functools.partial(middle_kernel, soft, factor),
         [shape(PANEL, sizes[1], dtype=BF16)] * 2
         + [shape(sizes[1], PANEL, dtype=BF16)] * 2
         + [shape(panels // 2, 4, PANEL, PANEL, dtype=BF16), shape(cols, total)],
         [SM] + [VM] * 5,
         [
             pltpu.VMEM((cols, total), F32),
-            pltpu.VMEM((EXTRA, half), F32),
+            pltpu.VMEM((DEPTH, half), BF16),
             pltpu.VMEM((2 * cols, half), BF16),
+            pltpu.VMEM((LANES, half), F32),
         ],
         8,
-    )(core, own, oth, vec, sub, acc)
+    )(core, own, oth, vec, left, acc)
     direction, residual, image, send, stats = call(
-        second_kernel,
+        functools.partial(second_kernel, factor),
         [shape(cols, total), shape(cols, half), shape(cols, half), shape(cols, half + LANES), shape(2, cols, LANES)],
         [SM] + [VM] * 13,
         [

time: 52.3 us -> 49.7 us (0.950)
  Pallas kernels: 18 us -> 15.3 us
    pallas_call x4, Pallas kernels: 17 us -> 14.3 us  [the longest x1 5.12 us: by_columns(): call(functools.partial(second_kernel, factor), [shape(cols, total), shape...]
  transfers between devices with their start and end apart: 3 -> 3, of which waited for: 2 -> 2; matrix products, arithmetic and copies ran while one was open for 0% -> 0% of each run, Pallas kernels for 11% -> 8%
where the time goes in v5:
time: 49.7 us; the launch traced here: 49.5 us
  blocking collectives  30.3 us (61%)
  Pallas kernels  15.3 us (31%)
  waiting for transfers between devices  2.16 us (4%)
  starting transfers between devices  1 us (2%)
  between operations  0.66 us (1%)
    all_to_all x1, blocking collectives, by_columns(): lax.all_to_all(packed, AXES, 0, 0, axis_index_groups=groups, tiled=True)  16.8 us
    all_to_all x1, blocking collectives, by_columns(): lax.all_to_all(mixed, AXES, 0, 0, axis_index_groups=groups, tiled=True)  13.6 us
    pallas_call x1, Pallas kernels, by_columns(): call(functools.partial(second_kernel, factor), [shape(cols, total), shape...  5.12 us
    pallas_call x1, Pallas kernels, by_columns(): call(functools.partial(first_kernel, soft, factor), [shape(PANEL, sizes[0...  4.17 us
    pallas_call x1, Pallas kernels, by_columns(): call(functools.partial(middle_kernel, soft, factor), [shape(PANEL, sizes[...  4.01 us
    ppermute x1, waiting for transfers between devices, by_columns(): lax.ppermute(mine, 'col', swap)  1.16 us
    pallas_call x1, Pallas kernels, by_columns(): call(functools.partial(pack_kernel, parts), [shape(parts, cols + EXTRA, L...  1.03 us
    ppermute x1, waiting for transfers between devices, by_columns(): come = lax.ppermute(send, 'col', swap)  1 us
  transfers between devices with their start and end apart: 3, of which 2 were waited for; matrix products, arithmetic and copies ran while one was open for 0% of the time, Pallas kernels for 8%

profile of v5, /device:TPU:0, one launch (start us, length us, event | category | flops | bytes accessed | tf_op | source)
XLA Modules:
  0.0 49.5 jit_solution(4736125624202853132)
XLA Ops:
  0.6 1.0 %shard_map.50 = f32[16,24,128]{2,1,0:T(8,128)S(1)} custom-call(f32[3,128]{1,0:T(4,128)} %pos_hbm.1, f32[1,128]{1,0:T(1,128)} %bitcast.2, f32[128,256]{1,0:T(8,128)} %rhs_hbm.1), custom_call_target="tpu_custom_call" | custom-call | tf_op jit(solution)/shard_map/pallas_call | solution.py:380
  1.7 16.8 %all_to_all.10.own_ref = f32[16,24,128]{2,1,0:T(8,128)S(1)} all-to-all(f32[16,24,128]{2,1,0:T(8,128)S(1)} %shard_map.50), channel_id=1, replica_groups={{0,2,4,6,8,10,12,14,16,18,20,22,24,26,28,30},{1,3,5,7,9,11,13,15,17,19,..., dimensions={0} | all-to-all | bytes 393216 | tf_op jit(solution)/shard_map/all_to_all | solution.py:391
  18.4 0.0 collective-permute-start
  18.4 4.2 %shard_map.51 = (bf16[256,9216]{1,0:T(8,128)(2,1)S(1)}, bf16[256,9216]{1,0:T(8,128)(2,1)S(1)}, bf16[7168,256]{1,0:T(8,128)(2,1)S(1)}, bf16[7168,256]{1,0:T(8,128...) custom-call(f32[16,24,128]{2,1,0:T(8,128)S(1)} %all_to_all.10.own_ref), custom_call_target="tpu_custom_call" | custom-call | tf_op jit(solution)/shard_map/pallas_call | solution.py:394
  22.6 0.0 collective-permute-done.oth_ref
  22.6 4.0 %shard_map.52 = (bf16[256,7168]{1,0:T(8,128)(2,1)S(1)}, bf16[256,7168]{1,0:T(8,128)(2,1)S(1)}, bf16[7168,256]{1,0:T(8,128)(2,1)S(1)}, bf16[7168,256]{1,0:T(8,128...) custom-call(s32[1]{0:T(128)} %bitcast.1.core_ref, f32[16,24,128]{2,1,0:T(8,128)S(1)} %all_to_all.10.own_ref, ...), custom_call_target="tpu_custom_call" | custom-call | tf_op jit(solution)/shard_map/pallas_call | solution.py:403
  26.6 0.6 %collective-permute-start.1 = (f32[16,4096]{1,0:T(8,128)S(1)}, f32[16,4096]{1,0:T(8,128)S(1)}, u32[]{:S(2)}, u32[]{:S(2)}) collective-permute-start(f32[16,4096]{1,0:T(8,128)S(1)} %get-tuple-element.23.mine_ref), channel_id=1, source_target_pairs={{0,1},{1,0},{2,3},{3,2},{4,5},{5,4},{6,7},{7,6},{8,9},{9,8},{10,11... | collective-permute-start | bytes 786440 | tf_op jit(solution)/shard_map/ppermute | solution.py:426
  27.2 1.2 %collective-permute-done.1.theirs_ref = f32[16,4096]{1,0:T(8,128)S(1)} collective-permute-done((f32[16,4096]{1,0:T(8,128)S(1)}, f32[16,4096]{1,0:T(8,128)S(1)}, u32[]{:S(2)}, u32[]{:S(2)}) %collective-permute-start.1) | collective-permute-done | bytes 262176 | tf_op jit(solution)/shard_map/ppermute | solution.py:426
  28.3 5.1 %shard_map.53 = (f32[16,4096]{1,0:T(8,128)S(1)}, f32[16,2048]{1,0:T(8,128)S(1)}, f32[16,2048]{1,0:T(8,128)S(1)}, f32[16,2176]{1,0:T(8,128)S(1)}, f32[2,16,128]{2,1,0:T(8,128)S(1)}) custom-call(s32[1]{0:T(128)} %bitcast.1.core_ref, f32[16,24,128]{2,1,0:T(8,128)S(1)} %all_to_all.10.own_ref, f32[16,24,128]{2,1,0:T(8,128)S(1)} %collective-permute-done.oth_ref, ...), custom_call_target="tpu_custom_call" | custom-call | tf_op jit(solution)/shard_map/pallas_call | solution.py:417
  33.5 0.4 collective-permute-start.2
  33.9 1.0 %collective-permute-done.2.come_ref = f32[16,2176]{1,0:T(8,128)S(1)} collective-permute-done((f32[16,2176]{1,0:T(8,128)S(1)}, f32[16,2176]{1,0:T(8,128)S(1)}, u32[]{:S(2)}, u32[]{:S(2)}) %collective-permute-start.2) | collective-permute-done | bytes 139296 | tf_op jit(solution)/shard_map/ppermute | solution.py:427
  34.9 0.2 shard_map.54
  35.1 13.6 %all_to_all.11.in_ref = f32[16,32,128]{2,1,0:T(8,128)S(1)} all-to-all(f32[16,32,128]{2,1,0:T(8,128)S(1)} %shard_map.54), channel_id=1, replica_groups={{0,2,4,6,8,10,12,14,16,18,20,22,24,26,28,30},{1,3,5,7,9,11,13,15,17,19,..., dimensions={0} | all-to-all | bytes 524288 | tf_op jit(solution)/shard_map/all_to_all | solution.py:431
  48.7 0.8 %shard_map.55 = (f32[128,256]{1,0:T(8,128)}, f32[128,256]{1,0:T(8,128)}) custom-call(f32[16,32,128]{2,1,0:T(8,128)S(1)} %all_to_all.11.in_ref), custom_call_target="tpu_custom_call" | custom-call | tf_op jit(solution)/shard_map/pallas_call | solution.py:432
Async XLA Ops:
  18.4 4.2 %collective-permute-start = (f32[16,24,128]{2,1,0:T(8,128)S(1)}, f32[16,24,128]{2,1,0:T(8,128)S(1)}, u32[]{:S(2)}, u32[]{:S(2)}) collective-permute-start(f32[16,24,128]{2,1,0:T(8,128)S(1)} %all_to_all.10.own_ref), channel_id=1, source_target_pairs={{0,1},{1,0},{2,3},{3,2},{4,5},{5,4},{6,7},{7,6},{8,9},{9,8},{10,11... | collective-permute-start | bytes 589832 | tf_op jit(solution)/shard_map/ppermute | solution.py:392
  26.6 1.7 %collective-permute-start.1 = (f32[16,4096]{1,0:T(8,128)S(1)}, f32[16,4096]{1,0:T(8,128)S(1)}, u32[]{:S(2)}, u32[]{:S(2)}) collective-permute-start(f32[16,4096]{1,0:T(8,128)S(1)} %get-tuple-element.23.mine_ref), channel_id=1, source_target_pairs={{0,1},{1,0},{2,3},{3,2},{4,5},{5,4},{6,7},{7,6},{8,9},{9,8},{10,11... | collective-permute-start | bytes 786440 | tf_op jit(solution)/shard_map/ppermute | solution.py:426
  33.5 1.4 %collective-permute-start.2 = (f32[16,2176]{1,0:T(8,128)S(1)}, f32[16,2176]{1,0:T(8,128)S(1)}, u32[]{:S(2)}, u32[]{:S(2)}) collective-permute-start(f32[16,2176]{1,0:T(8,128)S(1)} %get-tuple-element.36.send_ref), channel_id=1, source_target_pairs={{0,1},{1,0},{2,3},{3,2},{4,5},{5,4},{6,7},{7,6},{8,9},{9,8},{10,11... | collective-permute-start | bytes 417800 | tf_op jit(solution)/shard_map/ppermute | solution.py:427

commit v6 on v5

--- a/solution.py
+++ b/solution.py
@@ -12,10 +12,11 @@
 F32 = jnp.float32
 BF16 = jnp.bfloat16
 LANES = 128
-EXTRA = 8
+EXTRA = 4
 PANEL = 256
 WIDE = 1024
 AHEAD = 2
+COPIES = 4
 DEPTH = 48
 VM = pl.BlockSpec(memory_space=pltpu.VMEM)
 SM = pl.BlockSpec(memory_space=pltpu.SMEM)
@@ -86,22 +87,20 @@
 
 
 def pack_kernel(parts, pos_hbm, rad_hbm, rhs_hbm, out_ref, pos_ref, rad_ref, rhs_ref, sems):
-    copies = [
-        pltpu.make_async_copy(src, dst, sems.at[n])
-        for n, (src, dst) in enumerate(((rhs_hbm, rhs_ref), (pos_hbm, pos_ref), (rad_hbm, rad_ref)))
-    ]
+    rows = [pl.ds(n * (LANES // COPIES), LANES // COPIES) for n in range(COPIES)]
+    ends = [(rhs_hbm.at[at], rhs_ref.at[at]) for at in rows] + [(pos_hbm, pos_ref), (rad_hbm, rad_ref)]
+    copies = [pltpu.make_async_copy(src, dst, sems.at[n]) for n, (src, dst) in enumerate(ends)]
     for copy in copies:
         copy.start()
     for copy in copies:
         copy.wait()
     cols = rhs_ref.shape[1] // parts
     flipped = rhs_ref[...].T
-    extra = jnp.concatenate(
-        [pos_ref[...], rad_ref[...], jnp.zeros((EXTRA - 4, LANES), F32)], axis=0
-    )
+    extra = jnp.concatenate([pos_ref[...], rad_ref[...]], axis=0)
     for q in range(parts):
-        out_ref[q, 0:cols, :] = flipped[q * cols : (q + 1) * cols, :]
-        out_ref[q, cols : cols + EXTRA, :] = extra
+        for n in range(cols // EXTRA):
+            out_ref[q, n] = flipped[q * cols + n * EXTRA : q * cols + (n + 1) * EXTRA, :]
+        out_ref[q, cols // EXTRA] = extra
 
 
 def split(values):
@@ -134,9 +133,9 @@
     return out
 
 
-def factors(ref, soft, fact_ref, right_ref, left_ref=None):
-    parts, cols = ref.shape[0], ref.shape[1] - EXTRA
-    place = jnp.concatenate([ref[q, cols : cols + 3, :] for q in range(parts)], axis=1) * 512.0 - 256.0
+def factors(flat_ref, soft, fact_ref, right_ref, left_ref=None):
+    cols = flat_ref.shape[0] - EXTRA
+    place = flat_ref[cols : cols + 3, :] * 512.0 - 256.0
     whole = jnp.floor(place + 0.5)
     rest, more = pieces(place - whole, 2)
     both = rest + more
@@ -150,22 +149,23 @@
             fact_ref[at : at + row.shape[0], :] = row
             at += row.shape[0]
 
-    fact_ref[...] = jnp.zeros_like(fact_ref)
+    fact_ref[32:, :] = jnp.zeros_like(fact_ref[32:, :])
     twice, less, least = -2.0 * whole, -2.0 * rest, -2.0 * more
     write([twice, one, one, one, *norm, one, one, one, *pieces(cross + soft, 3), less, least, twice, twice, less, least, less])
-    right_ref[...] = fact_ref[0 : right_ref.shape[0], :].astype(BF16)
+    right_ref[...] = fact_ref[...].astype(BF16)
     if left_ref is not None:
         write([whole, *norm, one, one, one, *pieces(cross, 3), one, one, one, whole, whole, rest, more, rest, rest, more])
-        for q in range(parts):
+        for q in range(flat_ref.shape[1] // LANES):
             at = slice(q * LANES, (q + 1) * LANES)
-            left_ref[at, :] = fact_ref[:, at].T[:, 0 : left_ref.shape[1]].astype(BF16)
-
-
-def unpack(factor, ref, vec_ref):
-    parts, cols = ref.shape[0], ref.shape[1] - EXTRA
-    for q in range(parts):
+            left_ref[at, :] = fact_ref[:, at].T.astype(BF16)
+
+
+def unpack(factor, ref, flat_ref, vec_ref):
+    cols = flat_ref.shape[0] - EXTRA
+    for q in range(ref.shape[0]):
         at = slice(q * LANES, (q + 1) * LANES)
-        high, low = split(ref[q, 0:cols, :] * factor)
+        flat_ref[:, at] = jnp.concatenate([ref[q, n] for n in range(ref.shape[1])], axis=0)
+        high, low = split(flat_ref[0:cols, at] * factor)
         vec_ref[0:cols, at] = high
         vec_ref[cols : 2 * cols, at] = low
 
@@ -186,10 +186,10 @@
     return spans
 
 
-def first_kernel(soft, factor, own_ref, high_ref, low_ref, high_t_ref, low_t_ref, vec_ref, left_ref, acc_ref, right_ref, fact_ref):
+def first_kernel(soft, factor, own_ref, high_ref, low_ref, high_t_ref, low_t_ref, vec_ref, left_ref, acc_ref, flat_ref, right_ref, fact_ref):
     panels = vec_ref.shape[1] // PANEL
-    unpack(factor, own_ref, vec_ref)
-    factors(own_ref, soft, fact_ref, right_ref, left_ref)
+    unpack(factor, own_ref, flat_ref, vec_ref)
+    factors(flat_ref, soft, fact_ref, right_ref, left_ref)
     acc_ref[...] = jnp.zeros_like(acc_ref)
     tasks = []
     for t, columns, start in near_spans(panels):
@@ -214,12 +214,12 @@
 
 
 def middle_kernel(soft, factor, core_ref, own_ref, oth_ref, vec_ref, left_ref, near_ref, *refs):
-    high_ref, low_ref, high_t_ref, low_t_ref, far_ref, image_ref, acc_ref, right_ref, vec_oth_ref, fact_ref = refs
-    parts, cols = own_ref.shape[0], own_ref.shape[1] - EXTRA
-    half = parts * LANES
+    high_ref, low_ref, high_t_ref, low_t_ref, far_ref, image_ref, flat_ref, acc_ref, right_ref, vec_oth_ref, fact_ref = refs
+    cols, half = own_ref.shape[0] - EXTRA, own_ref.shape[1]
+    parts = half // LANES
     panels = half // PANEL
-    unpack(factor, oth_ref, vec_oth_ref)
-    factors(oth_ref, soft, fact_ref, right_ref)
+    unpack(factor, oth_ref, flat_ref, vec_oth_ref)
+    factors(flat_ref, soft, fact_ref, right_ref)
     acc_ref[:, 0:half] = near_ref[...]
     acc_ref[:, half:] = jnp.zeros_like(near_ref)
     tasks = []
@@ -255,7 +255,7 @@
     evaluate(left_ref, right_ref, tasks)
     for q in range(parts):
         at = slice(q * LANES, (q + 1) * LANES)
-        here = own_ref[q, 0:cols, :] / own_ref[q, cols + 3 : cols + 4, :]
+        here = own_ref[0:cols, at] / own_ref[cols + 3 : cols + 4, at]
         image_ref[:, at] = acc_ref[:, at] + here
     image_ref[:, half:] = acc_ref[:, half:]
 
@@ -263,31 +263,31 @@
 def second_kernel(factor, core_ref, own_ref, oth_ref, mine_ref, theirs_ref, *refs):
     near, across, far_ref = refs[0:4], refs[4:8], refs[8]
     dir_ref, res_ref, image_ref, send_ref, stat_ref, vec_ref, acc_ref, sum_ref = refs[9:]
-    parts, cols = own_ref.shape[0], own_ref.shape[1] - EXTRA
-    half = parts * LANES
+    cols, half = own_ref.shape[0] - EXTRA, own_ref.shape[1]
+    parts = half // LANES
     panels = half // PANEL
     sum_ref[:, 0:half] = mine_ref[:, 0:half] + theirs_ref[:, half:]
     sum_ref[:, half:] = mine_ref[:, half:] + theirs_ref[:, 0:half]
     blocks = [
-        (ref, q, slice(h * half + q * LANES, h * half + (q + 1) * LANES))
+        (ref, slice(q * LANES, (q + 1) * LANES), slice(h * half + q * LANES, h * half + (q + 1) * LANES))
         for h, ref in enumerate((own_ref, oth_ref))
         for q in range(parts)
     ]
     zero = jnp.zeros((cols, LANES), F32)
     norm, curve, fresh = zero, zero, zero
     for ref, q, at in blocks:
-        value = ref[q, 0:cols, :]
+        value = ref[0:cols, q]
         norm = norm + value * value
         curve = curve + value * sum_ref[:, at]
     norm = jnp.sum(norm, axis=1, keepdims=True)
     step = norm / jnp.sum(curve, axis=1, keepdims=True)
     for ref, q, at in blocks:
-        value = ref[q, 0:cols, :] - step * sum_ref[:, at]
+        value = ref[0:cols, q] - step * sum_ref[:, at]
         fresh = fresh + value * value
     fresh = jnp.sum(fresh, axis=1, keepdims=True)
     ratio = fresh / norm
     for n, (ref, q, at) in enumerate(blocks):
-        value = ref[q, 0:cols, :]
+        value = ref[0:cols, q]
         left = value - step * sum_ref[:, at]
         direction = left + ratio * value
         if n < parts:
@@ -319,7 +319,7 @@
         direction = dir_ref[:, at]
         image = acc_ref[:, at]
         if n < parts:
-            image = image + direction / own_ref[q, cols + 3 : cols + 4, :]
+            image = image + direction / own_ref[cols + 3 : cols + 4, q]
             image_ref[:, at] = image
         else:
             send_ref[:, at.start - half : at.stop - half] = image
@@ -330,33 +330,38 @@
 
 
 def last_kernel(own_ref, dir_ref, res_ref, image_ref, send_ref, come_ref, stat_ref, out_ref):
-    parts, cols = own_ref.shape[0], own_ref.shape[1] - EXTRA
-    half = parts * LANES
+    cols, half = own_ref.shape[0] - EXTRA, own_ref.shape[1]
+    parts = half // LANES
     curve = jnp.sum(send_ref[:, half:] + come_ref[:, half:], axis=1, keepdims=True)
     first = stat_ref[0, :, 0:1]
     step = stat_ref[1, :, 0:1] / curve
     for q in range(parts):
         at = slice(q * LANES, (q + 1) * LANES)
-        out_ref[q, 0:cols, :] = first * own_ref[q, 0:cols, :] + step * dir_ref[:, at]
+        out_ref[q, 0:cols, :] = first * own_ref[0:cols, at] + step * dir_ref[:, at]
         out_ref[q, cols : 2 * cols, :] = res_ref[:, at] - step * (image_ref[:, at] + come_ref[:, at])
 
 
-def unpack_kernel(in_ref, sol_ref, res_ref):
+def unpack_kernel(in_ref, sol_hbm, res_hbm, sol_ref, res_ref, sems):
     parts, cols = in_ref.shape[0], in_ref.shape[1] // 2
-    sol_ref[...] = in_ref[:, 0:cols, :].reshape(parts * cols, LANES).T
-    res_ref[...] = in_ref[:, cols : 2 * cols, :].reshape(parts * cols, LANES).T
+    copies = []
+    for n, (ref, out) in enumerate(((sol_ref, sol_hbm), (res_ref, res_hbm))):
+        ref[...] = in_ref[:, n * cols : (n + 1) * cols, :].reshape(parts * cols, LANES).T
+        copies.append(pltpu.make_async_copy(ref, out, sems.at[n]))
+        copies[-1].start()
+    for copy in copies:
+        copy.wait()
 
 
 def shape(*dims, dtype=F32):
     return jax.ShapeDtypeStruct(dims, dtype)
 
 
-def call(kernel, out, ins, scratch=(), limit=8):
+def call(kernel, out, ins, scratch=(), limit=8, where=VM):
     return pl.pallas_call(
         kernel,
         out_shape=out,
         in_specs=ins,
-        out_specs=[VM] * len(out),
+        out_specs=[where] * len(out),
         scratch_shapes=list(scratch),
         compiler_params=pltpu.CompilerParams(vmem_limit_bytes=limit << 20),
     )
@@ -379,41 +384,41 @@
 
     (packed,) = call(
         functools.partial(pack_kernel, parts),
-        [shape(parts, cols + EXTRA, LANES)],
+        [shape(parts, cols // EXTRA + 1, EXTRA, LANES)],
         [pl.BlockSpec(memory_space=pltpu.HBM)] * 3,
         [
             pltpu.VMEM((3, LANES), F32),
             pltpu.VMEM((1, LANES), F32),
             pltpu.VMEM((LANES, columns), F32),
-            pltpu.SemaphoreType.DMA((3,)),
+            pltpu.SemaphoreType.DMA((COPIES + 2,)),
         ],
     )(*[pltpu.with_memory_space_constraint(x, pltpu.HBM) for x in (positions, radii.reshape(1, -1), right_side)])
     own = lax.all_to_all(packed, AXES, 0, 0, axis_index_groups=groups, tiled=True)
     oth = lax.ppermute(own, "col", swap)
     sizes = [sum(cs.stop - cs.start for _, cs, _ in spans(panels)) for spans in (near_spans, across_spans)]
-    *near, vec, left, acc = call(
+    *near, vec, left, acc, own_flat = call(
         functools.partial(first_kernel, soft, factor),
         [shape(PANEL, sizes[0], dtype=BF16)] * 2
         + [shape(sizes[0] - half, PANEL, dtype=BF16)] * 2
-        + [shape(2 * cols, half, dtype=BF16), shape(half, DEPTH, dtype=BF16), shape(cols, half)],
+        + [shape(2 * cols, half, dtype=BF16), shape(half, DEPTH, dtype=BF16), shape(cols, half), shape(cols + EXTRA, half)],
         [VM],
-        [pltpu.VMEM((DEPTH, half), BF16), pltpu.VMEM((LANES, half), F32)],
+        [pltpu.VMEM((DEPTH, half), BF16), pltpu.VMEM((DEPTH, half), F32)],
         16,
     )(own)
-    *across, mine = call(
+    *across, mine, oth_flat = call(
         functools.partial(middle_kernel, soft, factor),
         [shape(PANEL, sizes[1], dtype=BF16)] * 2
         + [shape(sizes[1], PANEL, dtype=BF16)] * 2
-        + [shape(panels // 2, 4, PANEL, PANEL, dtype=BF16), shape(cols, total)],
+        + [shape(panels // 2, 4, PANEL, PANEL, dtype=BF16), shape(cols, total), shape(cols + EXTRA, half)],
         [SM] + [VM] * 5,
         [
             pltpu.VMEM((cols, total), F32),
             pltpu.VMEM((DEPTH, half), BF16),
             pltpu.VMEM((2 * cols, half), BF16),
-            pltpu.VMEM((LANES, half), F32),
+            pltpu.VMEM((DEPTH, half), F32),
         ],
         8,
-    )(core, own, oth, vec, left, acc)
+    )(core, own_flat, oth, vec, left, acc)
     direction, residual, image, send, stats = call(
         functools.partial(second_kernel, factor),
         [shape(cols, total), shape(cols, half), shape(cols, half), shape(cols, half + LANES), shape(2, cols, LANES)],
@@ -423,13 +428,14 @@
             pltpu.VMEM((cols, total), F32),
             pltpu.VMEM((cols, total), F32),
         ],
-    )(core, own, oth, mine, lax.ppermute(mine, "col", swap), *near, *across)
+    )(core, own_flat, oth_flat, mine, lax.ppermute(mine, "col", swap), *near, *across)
     come = lax.ppermute(send, "col", swap)
     (mixed,) = call(last_kernel, [shape(parts, 2 * cols, LANES)], [VM] * 7)(
-        own, direction, residual, image, send, come, stats
+        own_flat, direction, residual, image, send, come, stats
     )
     mixed = lax.all_to_all(mixed, AXES, 0, 0, axis_index_groups=groups, tiled=True)
-    return tuple(call(unpack_kernel, [shape(LANES, columns)] * 2, [VM])(mixed))
+    turned = [pltpu.VMEM((LANES, columns), F32)] * 2 + [pltpu.SemaphoreType.DMA((2,))]
+    return tuple(call(unpack_kernel, [shape(LANES, columns)] * 2, [VM], turned, where=pl.BlockSpec(memory_space=pltpu.HBM))(mixed))
 
 
 def body(positions, radii, right_side):

time: 49.7 us -> 49 us (0.986)
  blocking collectives: 30.3 us -> 29.6 us
    all_to_all x1, blocking collectives: 16.8 us -> 16 us  [by_columns(): lax.all_to_all(packed, AXES, 0, 0, axis_index_groups=groups, tiled=True)]
  transfers between devices with their start and end apart: 3 -> 3, of which waited for: 2 -> 2; matrix products, arithmetic and copies ran while one was open for 0% -> 0% of each run, Pallas kernels for 8% -> 9%
where the time goes in v6:
time: 49 us; the launch traced here: 48.7 us
  blocking collectives  29.6 us (60%)
  Pallas kernels  15.3 us (31%)
  waiting for transfers between devices  2.16 us (4%)
  starting transfers between devices  1.01 us (2%)
  between operations  0.66 us (1%)
    all_to_all x1, blocking collectives, by_columns(): lax.all_to_all(packed, AXES, 0, 0, axis_index_groups=groups, tiled=True)  16 us
    all_to_all x1, blocking collectives, by_columns(): lax.all_to_all(mixed, AXES, 0, 0, axis_index_groups=groups, tiled=True)  13.6 us
    pallas_call x1, Pallas kernels, by_columns(): call(functools.partial(second_kernel, factor), [shape(cols, total), shape...  5.11 us
    pallas_call x1, Pallas kernels, by_columns(): call(functools.partial(first_kernel, soft, factor), [shape(PANEL, sizes[0...  4.18 us
    pallas_call x1, Pallas kernels, by_columns(): call(functools.partial(middle_kernel, soft, factor), [shape(PANEL, sizes[...  4.03 us
    ppermute x1, waiting for transfers between devices, by_columns(): lax.ppermute(mine, 'col', swap)  1.16 us
    ppermute x1, waiting for transfers between devices, by_columns(): come = lax.ppermute(send, 'col', swap)  1 us
  transfers between devices with their start and end apart: 3, of which 2 were waited for; matrix products, arithmetic and copies ran while one was open for 0% of the time, Pallas kernels for 9%

profile of v6, /device:TPU:0, one launch (start us, length us, event | category | flops | bytes accessed | tf_op | source)
XLA Modules:
  0.0 48.7 jit_solution(12849817016763298963)
XLA Ops:
  0.6 1.0 %shard_map.50 = f32[16,5,4,128]{3,2,1,0:T(4,128)S(1)} custom-call(f32[3,128]{1,0:T(4,128)} %pos_hbm.1, f32[1,128]{1,0:T(1,128)} %bitcast.2, f32[128,256]{1,0:T(8,128)} %rhs_hbm.1), custom_call_target="tpu_custom_call" | custom-call | tf_op jit(solution)/shard_map/pallas_call | solution.py:385
  1.6 16.0 %all_to_all.10.own_ref = f32[16,5,4,128]{3,2,1,0:T(4,128)S(1)} all-to-all(f32[16,5,4,128]{3,2,1,0:T(4,128)S(1)} %shard_map.50), channel_id=1, replica_groups={{0,2,4,6,8,10,12,14,16,18,20,22,24,26,28,30},{1,3,5,7,9,11,13,15,17,19,..., dimensions={0} | all-to-all | bytes 327680 | tf_op jit(solution)/shard_map/all_to_all | solution.py:396
  17.6 0.0 collective-permute-start
  17.7 4.2 %shard_map.51 = (bf16[256,9216]{1,0:T(8,128)(2,1)S(1)}, bf16[256,9216]{1,0:T(8,128)(2,1)S(1)}, bf16[7168,256]{1,0:T(8,128)(2,1)S(1)}, bf16[7168,256]{1,0:T(8,128...) custom-call(f32[16,5,4,128]{3,2,1,0:T(4,128)S(1)} %all_to_all.10.own_ref), custom_call_target="tpu_custom_call" | custom-call | tf_op jit(solution)/shard_map/pallas_call | solution.py:399
  21.8 0.0 collective-permute-done.oth_ref
  21.8 4.0 %shard_map.52 = (bf16[256,7168]{1,0:T(8,128)(2,1)S(1)}, bf16[256,7168]{1,0:T(8,128)(2,1)S(1)}, bf16[7168,256]{1,0:T(8,128)(2,1)S(1)}, bf16[7168,256]{1,0:T(8,128...) custom-call(s32[1]{0:T(128)} %bitcast.1.core_ref, ...), custom_call_target="tpu_custom_call" | custom-call | tf_op jit(solution)/shard_map/pallas_call | solution.py:408
  25.9 0.6 %collective-permute-start.1 = (f32[16,4096]{1,0:T(8,128)S(1)}, f32[16,4096]{1,0:T(8,128)S(1)}, u32[]{:S(2)}, u32[]{:S(2)}) collective-permute-start(f32[16,4096]{1,0:T(8,128)S(1)} %get-tuple-element.27.mine_ref), channel_id=1, source_target_pairs={{0,1},{1,0},{2,3},{3,2},{4,5},{5,4},{6,7},{7,6},{8,9},{9,8},{10,11... | collective-permute-start | bytes 786440 | tf_op jit(solution)/shard_map/ppermute | solution.py:431
  26.4 1.2 %collective-permute-done.1.theirs_ref = f32[16,4096]{1,0:T(8,128)S(1)} collective-permute-done((f32[16,4096]{1,0:T(8,128)S(1)}, f32[16,4096]{1,0:T(8,128)S(1)}, u32[]{:S(2)}, u32[]{:S(2)}) %collective-permute-start.1) | collective-permute-done | bytes 262176 | tf_op jit(solution)/shard_map/ppermute | solution.py:431
  27.6 5.1 %shard_map.53 = (f32[16,4096]{1,0:T(8,128)S(1)}, f32[16,2048]{1,0:T(8,128)S(1)}, f32[16,2048]{1,0:T(8,128)S(1)}, f32[16,2176]{1,0:T(8,128)S(1)}, f32[2,16,128]{2,1,0:T(8,128)S(1)}) custom-call(s32[1]{0:T(128)} %bitcast.1.core_ref, f32[20,2048]{1,0:T(8,128)S(1)} %get-tuple-element.22.own_ref, f32[20,2048]{1,0:T(8,128)S(1)} %get-tuple-element.26.oth_ref, ...), custom_call_target="tpu_custom_call" | custom-call | tf_op jit(solution)/shard_map/pallas_call | solution.py:422
  32.7 0.4 collective-permute-start.2
  33.2 1.0 %collective-permute-done.2.come_ref = f32[16,2176]{1,0:T(8,128)S(1)} collective-permute-done((f32[16,2176]{1,0:T(8,128)S(1)}, f32[16,2176]{1,0:T(8,128)S(1)}, u32[]{:S(2)}, u32[]{:S(2)}) %collective-permute-start.2) | collective-permute-done | bytes 139296 | tf_op jit(solution)/shard_map/ppermute | solution.py:432
  34.2 0.2 shard_map.54
  34.3 13.6 %all_to_all.11.in_ref = f32[16,32,128]{2,1,0:T(8,128)S(1)} all-to-all(f32[16,32,128]{2,1,0:T(8,128)S(1)} %shard_map.54), channel_id=1, replica_groups={{0,2,4,6,8,10,12,14,16,18,20,22,24,26,28,30},{1,3,5,7,9,11,13,15,17,19,..., dimensions={0} | all-to-all | bytes 524288 | tf_op jit(solution)/shard_map/all_to_all | solution.py:436
  47.9 0.8 %shard_map.55 = (f32[128,256]{1,0:T(8,128)}, f32[128,256]{1,0:T(8,128)}) custom-call(f32[16,32,128]{2,1,0:T(8,128)S(1)} %all_to_all.11.in_ref), custom_call_target="tpu_custom_call" | custom-call | tf_op jit(solution)/shard_map/pallas_call | solution.py:438
Async XLA Ops:
  17.6 4.2 %collective-permute-start = (f32[16,5,4,128]{3,2,1,0:T(4,128)S(1)}, f32[16,5,4,128]{3,2,1,0:T(4,128)S(1)}, u32[]{:S(2)}, u32[]{:S(2)}) collective-permute-start(f32[16,5,4,128]{3,2,1,0:T(4,128)S(1)} %all_to_all.10.own_ref), channel_id=1, source_target_pairs={{0,1},{1,0},{2,3},{3,2},{4,5},{5,4},{6,7},{7,6},{8,9},{9,8},{10,11... | collective-permute-start | bytes 491528 | tf_op jit(solution)/shard_map/ppermute | solution.py:397
  25.9 1.7 %collective-permute-start.1 = (f32[16,4096]{1,0:T(8,128)S(1)}, f32[16,4096]{1,0:T(8,128)S(1)}, u32[]{:S(2)}, u32[]{:S(2)}) collective-permute-start(f32[16,4096]{1,0:T(8,128)S(1)} %get-tuple-element.27.mine_ref), channel_id=1, source_target_pairs={{0,1},{1,0},{2,3},{3,2},{4,5},{5,4},{6,7},{7,6},{8,9},{9,8},{10,11... | collective-permute-start | bytes 786440 | tf_op jit(solution)/shard_map/ppermute | solution.py:431
  32.7 1.4 %collective-permute-start.2 = (f32[16,2176]{1,0:T(8,128)S(1)}, f32[16,2176]{1,0:T(8,128)S(1)}, u32[]{:S(2)}, u32[]{:S(2)}) collective-permute-start(f32[16,2176]{1,0:T(8,128)S(1)} %get-tuple-element.40.send_ref), channel_id=1, source_target_pairs={{0,1},{1,0},{2,3},{3,2},{4,5},{5,4},{6,7},{7,6},{8,9},{9,8},{10,11... | collective-permute-start | bytes 417800 | tf_op jit(solution)/shard_map/ppermute | solution.py:432

commit v7 on v6

--- a/solution.py
+++ b/solution.py
@@ -14,12 +14,13 @@
 LANES = 128
 EXTRA = 4
 PANEL = 256
-WIDE = 1024
-AHEAD = 2
+WIDE = 256
+DEEP, BROAD = 256, 256
+EARLY = 4
+AHEAD = 6
 COPIES = 4
 DEPTH = 48
 VM = pl.BlockSpec(memory_space=pltpu.VMEM)
-SM = pl.BlockSpec(memory_space=pltpu.SMEM)
 KERNEL_BYTES = 32 << 20
 
 
@@ -114,14 +115,14 @@
     return both[0:cols] + both[cols:] + jnp.dot(vec[0:cols], low, preferred_element_type=F32)
 
 
-def evaluate(left_ref, right_ref, tasks):
+def evaluate(left_ref, right_ref, tasks, ahead):
     begun = []
-    for n in range(len(tasks) + AHEAD):
+    for n in range(len(tasks) + ahead):
         if n < len(tasks):
             rows, at, _ = tasks[n]
             begun.append(jnp.dot(left_ref[rows, :], right_ref[:, at], preferred_element_type=F32))
-        if n >= AHEAD:
-            tasks[n - AHEAD][2](*split(lax.rsqrt(begun[n - AHEAD])))
+        if n >= ahead:
+            tasks[n - ahead][2](*split(lax.rsqrt(begun[n - ahead])))
 
 
 def pieces(values, count):
@@ -133,7 +134,7 @@
     return out
 
 
-def factors(flat_ref, soft, fact_ref, right_ref, left_ref=None):
+def factors(flat_ref, soft, fact_ref, right_ref=None, left_ref=None):
     cols = flat_ref.shape[0] - EXTRA
     place = flat_ref[cols : cols + 3, :] * 512.0 - 256.0
     whole = jnp.floor(place + 0.5)
@@ -151,8 +152,9 @@
 
     fact_ref[32:, :] = jnp.zeros_like(fact_ref[32:, :])
     twice, less, least = -2.0 * whole, -2.0 * rest, -2.0 * more
-    write([twice, one, one, one, *norm, one, one, one, *pieces(cross + soft, 3), less, least, twice, twice, less, least, less])
-    right_ref[...] = fact_ref[...].astype(BF16)
+    if right_ref is not None:
+        write([twice, one, one, one, *norm, one, one, one, *pieces(cross + soft, 3), less, least, twice, twice, less, least, less])
+        right_ref[...] = fact_ref[...].astype(BF16)
     if left_ref is not None:
         write([whole, *norm, one, one, one, *pieces(cross, 3), one, one, one, whole, whole, rest, more, rest, rest, more])
         for q in range(flat_ref.shape[1] // LANES):
@@ -178,15 +180,8 @@
     return spans
 
 
-def across_spans(panels):
-    spans, start = [], 0
-    for t in range(1, panels):
-        spans.append((t, slice(0, t * PANEL), start))
-        start += t * PANEL
-    return spans
-
-
-def first_kernel(soft, factor, own_ref, high_ref, low_ref, high_t_ref, low_t_ref, vec_ref, left_ref, acc_ref, flat_ref, right_ref, fact_ref):
+def first_kernel(soft, factor, own_ref, *refs):
+    high_ref, low_ref, high_t_ref, low_t_ref, right_ref, acc_ref, flat_ref, vec_ref, left_ref, fact_ref = refs
     panels = vec_ref.shape[1] // PANEL
     unpack(factor, own_ref, flat_ref, vec_ref)
     factors(flat_ref, soft, fact_ref, right_ref, left_ref)
@@ -210,135 +205,94 @@
                     acc_ref[:, rows] += product(vec_ref[:, at.start + skip : at.stop], high, low)
 
             tasks.append((rows, at, use))
-    evaluate(left_ref, right_ref, tasks)
-
-
-def middle_kernel(soft, factor, core_ref, own_ref, oth_ref, vec_ref, left_ref, near_ref, *refs):
-    high_ref, low_ref, high_t_ref, low_t_ref, far_ref, image_ref, flat_ref, acc_ref, right_ref, vec_oth_ref, fact_ref = refs
+    evaluate(left_ref, right_ref, tasks, AHEAD)
+
+
+def middle_kernel(soft, factor, own_ref, oth_ref, right_ref, near_ref, *refs):
+    high_ref, low_ref, image_ref, flat_ref, vec_ref, left_ref, fact_ref = refs
     cols, half = own_ref.shape[0] - EXTRA, own_ref.shape[1]
-    parts = half // LANES
-    panels = half // PANEL
-    unpack(factor, oth_ref, flat_ref, vec_oth_ref)
-    factors(flat_ref, soft, fact_ref, right_ref)
-    acc_ref[:, 0:half] = near_ref[...]
-    acc_ref[:, half:] = jnp.zeros_like(near_ref)
+    unpack(factor, oth_ref, flat_ref, vec_ref)
+    factors(flat_ref, soft, fact_ref, None, left_ref)
+    image_ref[...] = near_ref[...] + own_ref[0:cols, :] / own_ref[cols + 3 : cols + 4, :]
     tasks = []
-    for n in range(panels // 2):
-        place = pl.multiple_of((core_ref[0] * (panels // 2) + n) * PANEL, PANEL)
-        rows, there = pl.ds(place, PANEL), pl.ds(pl.multiple_of(half + place, PANEL), PANEL)
-
-        def use_far(high, low, n=n, rows=rows, there=there):
-            far_ref[n, 0] = high
-            far_ref[n, 1] = low
-            acc_ref[:, there] += product(vec_ref[:, rows], high, low)
-            high, low = high.T, low.T
-            far_ref[n, 2] = high
-            far_ref[n, 3] = low
-            acc_ref[:, rows] += product(vec_oth_ref[:, rows], high, low)
-
-        tasks.append((rows, rows, use_far))
-    for t, columns, start in across_spans(panels):
-        rows = slice(t * PANEL, (t + 1) * PANEL)
-        for c in range(columns.start, columns.stop, WIDE):
-            at = slice(c, min(c + WIDE, columns.stop))
-
-            def use(high, low, rows=rows, at=at, to=slice(start + c, start + at.stop)):
-                high_ref[:, to] = high
-                low_ref[:, to] = low
-                acc_ref[:, half + at.start : half + at.stop] += product(vec_ref[:, rows], high, low)
-                high, low = high.T, low.T
-                high_t_ref[to, :] = high
-                low_t_ref[to, :] = low
-                acc_ref[:, rows] += product(vec_oth_ref[:, at], high, low)
+    for r in range(0, half, DEEP):
+        rows = slice(r, r + DEEP)
+        for c in range(0, half, BROAD):
+            at = slice(c, min(c + BROAD, half))
+
+            def use(high, low, rows=rows, at=at):
+                high_ref[rows, at] = high
+                low_ref[rows, at] = low
+                image_ref[:, at] += product(vec_ref[:, rows], high, low)
 
             tasks.append((rows, at, use))
-    evaluate(left_ref, right_ref, tasks)
-    for q in range(parts):
-        at = slice(q * LANES, (q + 1) * LANES)
-        here = own_ref[0:cols, at] / own_ref[cols + 3 : cols + 4, at]
-        image_ref[:, at] = acc_ref[:, at] + here
-    image_ref[:, half:] = acc_ref[:, half:]
-
-
-def second_kernel(factor, core_ref, own_ref, oth_ref, mine_ref, theirs_ref, *refs):
-    near, across, far_ref = refs[0:4], refs[4:8], refs[8]
-    dir_ref, res_ref, image_ref, send_ref, stat_ref, vec_ref, acc_ref, sum_ref = refs[9:]
-    cols, half = own_ref.shape[0] - EXTRA, own_ref.shape[1]
-    parts = half // LANES
-    panels = half // PANEL
-    sum_ref[:, 0:half] = mine_ref[:, 0:half] + theirs_ref[:, half:]
-    sum_ref[:, half:] = mine_ref[:, half:] + theirs_ref[:, 0:half]
-    blocks = [
-        (ref, slice(q * LANES, (q + 1) * LANES), slice(h * half + q * LANES, h * half + (q + 1) * LANES))
-        for h, ref in enumerate((own_ref, oth_ref))
-        for q in range(parts)
-    ]
+    evaluate(left_ref, right_ref, tasks, EARLY)
+
+
+def near_kernel(factor, image_ref, high_ref, low_ref, high_t_ref, low_t_ref, out_ref, vec_ref):
+    cols, half = image_ref.shape
+    for c in range(0, half, LANES):
+        at = slice(c, c + LANES)
+        vec_ref[0:cols, at], vec_ref[cols : 2 * cols, at] = split(image_ref[:, at] * factor)
+    out_ref[...] = jnp.zeros_like(out_ref)
+    for t, columns, start in near_spans(half // PANEL):
+        rows, after = slice(t * PANEL, (t + 1) * PANEL), slice((t + 1) * PANEL, half)
+        to = slice(start, start + half - rows.start)
+        out_ref[:, columns] += product(vec_ref[:, rows], high_ref[:, to], low_ref[:, to])
+        if after.start < half:
+            to = slice(start - rows.start, start - rows.start + half - after.start)
+            out_ref[:, rows] += product(vec_ref[:, after], high_t_ref[to, :], low_t_ref[to, :])
+
+
+def second_kernel(factor, own_ref, oth_ref, im_own_ref, im_oth_ref, near_ref, high_ref, low_ref, *refs):
+    dir_ref, res_ref, image_ref, curve_ref, stat_ref, vec_ref, acc_ref = refs
+    cols, half = im_own_ref.shape
+    places = [slice(c, c + LANES) for c in range(0, half, LANES)]
+    for at in places:
+        vec_ref[0:cols, at], vec_ref[cols : 2 * cols, at] = split(im_oth_ref[:, at] * factor)
+    acc_ref[...] = near_ref[...] + im_own_ref[...] / own_ref[cols + 3 : cols + 4, :]
+    for r in range(0, half, PANEL):
+        rows = slice(r, r + PANEL)
+        acc_ref[...] += product(vec_ref[:, rows], high_ref[rows, :], low_ref[rows, :])
+    blocks = [(ref, im, at) for ref, im in ((own_ref, im_own_ref), (oth_ref, im_oth_ref)) for at in places]
     zero = jnp.zeros((cols, LANES), F32)
     norm, curve, fresh = zero, zero, zero
-    for ref, q, at in blocks:
-        value = ref[0:cols, q]
+    for ref, im, at in blocks:
+        value = ref[0:cols, at]
         norm = norm + value * value
-        curve = curve + value * sum_ref[:, at]
+        curve = curve + value * im[:, at]
     norm = jnp.sum(norm, axis=1, keepdims=True)
     step = norm / jnp.sum(curve, axis=1, keepdims=True)
-    for ref, q, at in blocks:
-        value = ref[0:cols, q] - step * sum_ref[:, at]
+    for ref, im, at in blocks:
+        value = ref[0:cols, at] - step * im[:, at]
         fresh = fresh + value * value
     fresh = jnp.sum(fresh, axis=1, keepdims=True)
     ratio = fresh / norm
-    for n, (ref, q, at) in enumerate(blocks):
-        value = ref[0:cols, q]
-        left = value - step * sum_ref[:, at]
+    curve = zero
+    for at in places:
+        value, first = own_ref[0:cols, at], im_own_ref[:, at]
+        left = value - step * first
         direction = left + ratio * value
-        if n < parts:
-            res_ref[:, at] = left
+        image = first + (ratio * first - step * acc_ref[:, at])
+        res_ref[:, at] = left
         dir_ref[:, at] = direction
-        high, low = split(direction * factor)
-        vec_ref[0:cols, at] = high
-        vec_ref[cols : 2 * cols, at] = low
-    acc_ref[...] = jnp.zeros_like(acc_ref)
-    for t, columns, start in near_spans(panels):
-        rows, after = slice(t * PANEL, (t + 1) * PANEL), slice((t + 1) * PANEL, half)
-        to = slice(start, start + half - rows.start)
-        acc_ref[:, columns] += product(vec_ref[:, rows], near[0][:, to], near[1][:, to])
-        if after.start < half:
-            to = slice(start - rows.start, start - rows.start + half - after.start)
-            acc_ref[:, rows] += product(vec_ref[:, after], near[2][to, :], near[3][to, :])
-    for t, columns, start in across_spans(panels):
-        rows, there = slice(t * PANEL, (t + 1) * PANEL), slice(half, half + columns.stop)
-        to = slice(start, start + columns.stop)
-        acc_ref[:, there] += product(vec_ref[:, rows], across[0][:, to], across[1][:, to])
-        acc_ref[:, rows] += product(vec_ref[:, there], across[2][to, :], across[3][to, :])
-    for n in range(panels // 2):
-        place = pl.multiple_of((core_ref[0] * (panels // 2) + n) * PANEL, PANEL)
-        rows, at = pl.ds(place, PANEL), pl.ds(pl.multiple_of(half + place, PANEL), PANEL)
-        acc_ref[:, at] += product(vec_ref[:, rows], far_ref[n, 0], far_ref[n, 1])
-        acc_ref[:, rows] += product(vec_ref[:, at], far_ref[n, 2], far_ref[n, 3])
-    curve = zero
-    for n, (ref, q, at) in enumerate(blocks):
-        direction = dir_ref[:, at]
-        image = acc_ref[:, at]
-        if n < parts:
-            image = image + direction / own_ref[cols + 3 : cols + 4, q]
-            image_ref[:, at] = image
-        else:
-            send_ref[:, at.start - half : at.stop - half] = image
+        image_ref[:, at] = image
         curve = curve + direction * image
-    send_ref[:, half:] = curve
+    curve_ref[...] = curve
     stat_ref[0] = jnp.broadcast_to(step, (cols, LANES))
     stat_ref[1] = jnp.broadcast_to(fresh, (cols, LANES))
 
 
-def last_kernel(own_ref, dir_ref, res_ref, image_ref, send_ref, come_ref, stat_ref, out_ref):
+def last_kernel(own_ref, dir_ref, res_ref, image_ref, curve_ref, other_ref, stat_ref, out_ref):
     cols, half = own_ref.shape[0] - EXTRA, own_ref.shape[1]
     parts = half // LANES
-    curve = jnp.sum(send_ref[:, half:] + come_ref[:, half:], axis=1, keepdims=True)
+    curve = jnp.sum(curve_ref[...] + other_ref[...], axis=1, keepdims=True)
     first = stat_ref[0, :, 0:1]
     step = stat_ref[1, :, 0:1] / curve
     for q in range(parts):
         at = slice(q * LANES, (q + 1) * LANES)
         out_ref[q, 0:cols, :] = first * own_ref[0:cols, at] + step * dir_ref[:, at]
-        out_ref[q, cols : 2 * cols, :] = res_ref[:, at] - step * (image_ref[:, at] + come_ref[:, at])
+        out_ref[q, cols : 2 * cols, :] = res_ref[:, at] - step * image_ref[:, at]
 
 
 def unpack_kernel(in_ref, sol_hbm, res_hbm, sol_ref, res_ref, sems):
@@ -380,7 +334,6 @@
     soft, factor = softening * 4.0**9, kernel_scale * 2.0**9
     groups = [[2 * chip + core for chip in range(parts)] for core in range(2)]
     swap = [(i, i ^ 1) for i in range(col_size)]
-    core = (lax.axis_index("col") % 2).astype(jnp.int32).reshape(1)
 
     (packed,) = call(
         functools.partial(pack_kernel, parts),
@@ -395,43 +348,42 @@
     )(*[pltpu.with_memory_space_constraint(x, pltpu.HBM) for x in (positions, radii.reshape(1, -1), right_side)])
     own = lax.all_to_all(packed, AXES, 0, 0, axis_index_groups=groups, tiled=True)
     oth = lax.ppermute(own, "col", swap)
-    sizes = [sum(cs.stop - cs.start for _, cs, _ in spans(panels)) for spans in (near_spans, across_spans)]
-    *near, vec, left, acc, own_flat = call(
+    size = sum(cs.stop - cs.start for _, cs, _ in near_spans(panels))
+    *near, right, acc, own_flat = call(
         functools.partial(first_kernel, soft, factor),
-        [shape(PANEL, sizes[0], dtype=BF16)] * 2
-        + [shape(sizes[0] - half, PANEL, dtype=BF16)] * 2
-        + [shape(2 * cols, half, dtype=BF16), shape(half, DEPTH, dtype=BF16), shape(cols, half), shape(cols + EXTRA, half)],
+        [shape(PANEL, size, dtype=BF16)] * 2
+        + [shape(size - half, PANEL, dtype=BF16)] * 2
+        + [shape(DEPTH, half, dtype=BF16), shape(cols, half), shape(cols + EXTRA, half)],
         [VM],
-        [pltpu.VMEM((DEPTH, half), BF16), pltpu.VMEM((DEPTH, half), F32)],
+        [
+            pltpu.VMEM((2 * cols, half), BF16),
+            pltpu.VMEM((half, DEPTH), BF16),
+            pltpu.VMEM((DEPTH, half), F32),
+        ],
         16,
     )(own)
-    *across, mine, oth_flat = call(
+    *across, image, oth_flat = call(
         functools.partial(middle_kernel, soft, factor),
-        [shape(PANEL, sizes[1], dtype=BF16)] * 2
-        + [shape(sizes[1], PANEL, dtype=BF16)] * 2
-        + [shape(panels // 2, 4, PANEL, PANEL, dtype=BF16), shape(cols, total), shape(cols + EXTRA, half)],
-        [SM] + [VM] * 5,
+        [shape(half, half, dtype=BF16)] * 2 + [shape(cols, half), shape(cols + EXTRA, half)],
+        [VM] * 4,
         [
-            pltpu.VMEM((cols, total), F32),
-            pltpu.VMEM((DEPTH, half), BF16),
             pltpu.VMEM((2 * cols, half), BF16),
+            pltpu.VMEM((half, DEPTH), BF16),
             pltpu.VMEM((DEPTH, half), F32),
         ],
-        8,
-    )(core, own_flat, oth, vec, left, acc)
-    direction, residual, image, send, stats = call(
+        10,
+    )(own_flat, oth, right, acc)
+    image_oth = lax.ppermute(image, "col", swap)
+    vec = pltpu.VMEM((2 * cols, half), BF16)
+    (begun,) = call(functools.partial(near_kernel, factor), [shape(cols, half)], [VM] * 5, [vec])(image, *near)
+    direction, residual, second, curve, stats = call(
         functools.partial(second_kernel, factor),
-        [shape(cols, total), shape(cols, half), shape(cols, half), shape(cols, half + LANES), shape(2, cols, LANES)],
-        [SM] + [VM] * 13,
-        [
-            pltpu.VMEM((2 * cols, total), BF16),
-            pltpu.VMEM((cols, total), F32),
-            pltpu.VMEM((cols, total), F32),
-        ],
-    )(core, own_flat, oth_flat, mine, lax.ppermute(mine, "col", swap), *near, *across)
-    come = lax.ppermute(send, "col", swap)
+        [shape(cols, half)] * 3 + [shape(cols, LANES), shape(2, cols, LANES)],
+        [VM] * 7,
+        [vec, pltpu.VMEM((cols, half), F32)],
+    )(own_flat, oth_flat, image, image_oth, begun, *across)
     (mixed,) = call(last_kernel, [shape(parts, 2 * cols, LANES)], [VM] * 7)(
-        own_flat, direction, residual, image, send, come, stats
+        own_flat, direction, residual, second, curve, lax.ppermute(curve, "col", swap), stats
     )
     mixed = lax.all_to_all(mixed, AXES, 0, 0, axis_index_groups=groups, tiled=True)
     turned = [pltpu.VMEM((LANES, columns), F32)] * 2 + [pltpu.SemaphoreType.DMA((2,))]

time: 49 us -> 47.4 us (0.967)
  waiting for transfers between devices: 2.16 us -> 1.16 us
    ppermute x2, waiting for transfers between devices: 2.16 us -> 1.16 us  [the longest x1 1.16 us: by_columns(): lax.ppermute(curve, 'col', swap)]
    pallas_call x3 -> x4, Pallas kernels: 13.3 us -> 13.3 us  [the longest x1 4.44 us: by_columns(): call(functools.partial(middle_kernel, soft, factor), [shape(half, half, d...]
  transfers between devices with their start and end apart: 3 -> 3, of which waited for: 2 -> 1; matrix products, arithmetic and copies ran while one was open for 0% -> 0% of each run, Pallas kernels for 9% -> 13%
where the time goes in v7:
time: 47.4 us; the launch traced here: 47.1 us
  blocking collectives  29.4 us (62%)
  Pallas kernels  15.3 us (32%)
  waiting for transfers between devices  1.16 us (2%)
  between operations  0.66 us (1%)
  starting transfers between devices  0.58 us (1%)
    all_to_all x1, blocking collectives, by_columns(): lax.all_to_all(packed, AXES, 0, 0, axis_index_groups=groups, tiled=True)  16 us
    all_to_all x1, blocking collectives, by_columns(): lax.all_to_all(mixed, AXES, 0, 0, axis_index_groups=groups, tiled=True)  13.4 us
    pallas_call x1, Pallas kernels, by_columns(): call(functools.partial(middle_kernel, soft, factor), [shape(half, half, d...  4.44 us
    pallas_call x1, Pallas kernels, by_columns(): call(functools.partial(first_kernel, soft, factor), [shape(PANEL, size, d...  3.88 us
    pallas_call x1, Pallas kernels, by_columns(): call(functools.partial(second_kernel, factor), [shape(cols, half)] * 3 +...  2.57 us
    pallas_call x1, Pallas kernels, by_columns(): call(functools.partial(near_kernel, factor), [shape(cols, half)], [VM] *...  2.42 us
    ppermute x1, waiting for transfers between devices, by_columns(): lax.ppermute(curve, 'col', swap)  1.16 us
    pallas_call x1, Pallas kernels, by_columns(): call(functools.partial(pack_kernel, parts), [shape(parts, cols // EXTRA +...  0.96 us
  transfers between devices with their start and end apart: 3, of which 1 were waited for; matrix products, arithmetic and copies ran while one was open for 0% of the time, Pallas kernels for 13%

profile of v7, /device:TPU:0, one launch (start us, length us, event | category | flops | bytes accessed | tf_op | source)
XLA Modules:
  0.0 47.1 jit_solution(15206059529979084044)
XLA Ops:
  0.6 1.0 %shard_map.50 = f32[16,5,4,128]{3,2,1,0:T(4,128)S(1)} custom-call(f32[3,128]{1,0:T(4,128)} %pos_hbm.1, f32[1,128]{1,0:T(1,128)} %bitcast.1, f32[128,256]{1,0:T(8,128)} %rhs_hbm.1), custom_call_target="tpu_custom_call" | custom-call | tf_op jit(solution)/shard_map/pallas_call | solution.py:338
  1.6 16.0 %all_to_all.10.own_ref = f32[16,5,4,128]{3,2,1,0:T(4,128)S(1)} all-to-all(f32[16,5,4,128]{3,2,1,0:T(4,128)S(1)} %shard_map.50), channel_id=1, replica_groups={{0,2,4,6,8,10,12,14,16,18,20,22,24,26,28,30},{1,3,5,7,9,11,13,15,17,19,..., dimensions={0} | all-to-all | bytes 327680 | tf_op jit(solution)/shard_map/all_to_all | solution.py:349
  17.6 0.0 collective-permute-start
  17.7 3.9 %shard_map.51 = (bf16[256,9216]{1,0:T(8,128)(2,1)S(1)}, bf16[256,9216]{1,0:T(8,128)(2,1)S(1)}, bf16[7168,256]{1,0:T(8,128)(2,1)S(1)}, bf16[7168,256]{1,0:T(8,128...) custom-call(f32[16,5,4,128]{3,2,1,0:T(4,128)S(1)} %all_to_all.10.own_ref), custom_call_target="tpu_custom_call" | custom-call | tf_op jit(solution)/shard_map/pallas_call | solution.py:352
  21.5 0.0 collective-permute-done.oth_ref
  21.5 4.4 %shard_map.52 = (bf16[2048,2048]{1,0:T(8,128)(2,1)S(1)}, bf16[2048,2048]{1,0:T(8,128)(2,1)S(1)}, f32[16,2048]{1,0:T(8,128)S(1)}, f32[20,2048]{1,0:T(8,128)S(1)}) custom-call(f32[20,2048]{1,0:T(8,128)S(1)} %get-tuple-element.18.own_ref, f32[16,5,4,128]{3,2,1,0:T(4,128)S(1)} %collective-permute-done.oth_ref, bf16[48,2048]{1,0:T(8,128)(2,1)S(1)} %get-tuple-element.19.right_ref, ...), custom_call_target="tpu_custom_call" | custom-call | tf_op jit(solution)/shard_map/pallas_call | solution.py:365
  26.0 0.5 %collective-permute-start.1 = (f32[16,2048]{1,0:T(8,128)S(1)}, f32[16,2048]{1,0:T(8,128)S(1)}, u32[]{:S(2)}, u32[]{:S(2)}) collective-permute-start(f32[16,2048]{1,0:T(8,128)S(1)} %get-tuple-element.22.image_ref.im_own_ref), channel_id=1, source_target_pairs={{0,1},{1,0},{2,3},{3,2},{4,5},{5,4},{6,7},{7,6},{8,9},{9,8},{10,11... | collective-permute-start | bytes 393224 | tf_op jit(solution)/shard_map/ppermute | solution.py:376
  26.5 2.4 %shard_map.53.near_ref = f32[16,2048]{1,0:T(8,128)S(1)} custom-call(f32[16,2048]{1,0:T(8,128)S(1)} %get-tuple-element.22.image_ref.im_own_ref, bf16[256,9216]{1,0:T(8,128)(2,1)S(1)} %get-tuple-element.23.high_ref, bf16[256,9216]{1,0:T(8,128)(2,1)S(1)} %get-tuple-element.24.low_ref, bf16[7168,256]{1,0:T(8,128)(2,1)S(1)} %get-tuple-element.25.high_t_ref, ...), custom_call_target="tpu_custom_call" | custom-call | tf_op jit(solution)/shard_map/pallas_call | solution.py:378
  28.9 0.0 collective-permute-done.1.im_oth_ref
  28.9 2.6 %shard_map.54 = (f32[16,2048]{1,0:T(8,128)S(1)}, f32[16,2048]{1,0:T(8,128)S(1)}, f32[16,2048]{1,0:T(8,128)S(1)}, f32[16,128]{1,0:T(8,128)S(1)}, f32[2,16,128]{2,1,0:T(8,128)S(1)}) custom-call(f32[20,2048]{1,0:T(8,128)S(1)} %get-tuple-element.18.own_ref, f32[20,2048]{1,0:T(8,128)S(1)} %get-tuple-element.21.oth_ref, ...), custom_call_target="tpu_custom_call" | custom-call | tf_op jit(solution)/shard_map/pallas_call | solution.py:379
  31.5 0.1 collective-permute-start.2
  31.6 1.2 %collective-permute-done.2.other_ref = f32[16,128]{1,0:T(8,128)S(1)} collective-permute-done((f32[16,128]{1,0:T(8,128)S(1)}, f32[16,128]{1,0:T(8,128)S(1)}, u32[]{:S(2)}, u32[]{:S(2)}) %collective-permute-start.2) | collective-permute-done | bytes 8224 | tf_op jit(solution)/shard_map/ppermute | solution.py:386
  32.7 0.2 shard_map.55
  32.9 13.4 %all_to_all.11.in_ref = f32[16,32,128]{2,1,0:T(8,128)S(1)} all-to-all(f32[16,32,128]{2,1,0:T(8,128)S(1)} %shard_map.55), channel_id=1, replica_groups={{0,2,4,6,8,10,12,14,16,18,20,22,24,26,28,30},{1,3,5,7,9,11,13,15,17,19,..., dimensions={0} | all-to-all | bytes 524288 | tf_op jit(solution)/shard_map/all_to_all | solution.py:388
  46.3 0.8 %shard_map.56 = (f32[128,256]{1,0:T(8,128)}, f32[128,256]{1,0:T(8,128)}) custom-call(f32[16,32,128]{2,1,0:T(8,128)S(1)} %all_to_all.11.in_ref), custom_call_target="tpu_custom_call" | custom-call | tf_op jit(solution)/shard_map/pallas_call | solution.py:390
Async XLA Ops:
  17.6 3.9 %collective-permute-start = (f32[16,5,4,128]{3,2,1,0:T(4,128)S(1)}, f32[16,5,4,128]{3,2,1,0:T(4,128)S(1)}, u32[]{:S(2)}, u32[]{:S(2)}) collective-permute-start(f32[16,5,4,128]{3,2,1,0:T(4,128)S(1)} %all_to_all.10.own_ref), channel_id=1, source_target_pairs={{0,1},{1,0},{2,3},{3,2},{4,5},{5,4},{6,7},{7,6},{8,9},{9,8},{10,11... | collective-permute-start | bytes 491528 | tf_op jit(solution)/shard_map/ppermute | solution.py:350
  26.0 2.9 %collective-permute-start.1 = (f32[16,2048]{1,0:T(8,128)S(1)}, f32[16,2048]{1,0:T(8,128)S(1)}, u32[]{:S(2)}, u32[]{:S(2)}) collective-permute-start(f32[16,2048]{1,0:T(8,128)S(1)} %get-tuple-element.22.image_ref.im_own_ref), channel_id=1, source_target_pairs={{0,1},{1,0},{2,3},{3,2},{4,5},{5,4},{6,7},{7,6},{8,9},{9,8},{10,11... | collective-permute-start | bytes 393224 | tf_op jit(solution)/shard_map/ppermute | solution.py:376
  31.5 1.2 %collective-permute-start.2 = (f32[16,128]{1,0:T(8,128)S(1)}, f32[16,128]{1,0:T(8,128)S(1)}, u32[]{:S(2)}, u32[]{:S(2)}) collective-permute-start(f32[16,128]{1,0:T(8,128)S(1)} %get-tuple-element.32.curve_ref), channel_id=1, source_target_pairs={{0,1},{1,0},{2,3},{3,2},{4,5},{5,4},{6,7},{7,6},{8,9},{9,8},{10,11... | collective-permute-start | bytes 24584 | tf_op jit(solution)/shard_map/ppermute | solution.py:386

commit v8 on v7

--- a/solution.py
+++ b/solution.py
@@ -119,7 +119,9 @@
     begun = []
     for n in range(len(tasks) + ahead):
         if n < len(tasks):
-            rows, at, _ = tasks[n]
+            rows, at, _, prepare = tasks[n]
+            if prepare is not None:
+                prepare()
             begun.append(jnp.dot(left_ref[rows, :], right_ref[:, at], preferred_element_type=F32))
         if n >= ahead:
             tasks[n - ahead][2](*split(lax.rsqrt(begun[n - ahead])))
@@ -134,9 +136,9 @@
     return out
 
 
-def factors(flat_ref, soft, fact_ref, right_ref=None, left_ref=None):
+def factors(flat_ref, at, soft, fact_ref, right_ref=None, left_ref=None):
     cols = flat_ref.shape[0] - EXTRA
-    place = flat_ref[cols : cols + 3, :] * 512.0 - 256.0
+    place = flat_ref[cols : cols + 3, at] * 512.0 - 256.0
     whole = jnp.floor(place + 0.5)
     rest, more = pieces(place - whole, 2)
     both = rest + more
@@ -145,26 +147,25 @@
     cross = jnp.sum((2.0 * whole + both) * both, axis=0, keepdims=True)
 
     def write(rows):
-        at = 0
+        place = 0
         for row in rows:
-            fact_ref[at : at + row.shape[0], :] = row
-            at += row.shape[0]
-
-    fact_ref[32:, :] = jnp.zeros_like(fact_ref[32:, :])
+            fact_ref[place : place + row.shape[0], at] = row
+            place += row.shape[0]
+
+    fact_ref[32:, at] = jnp.zeros_like(fact_ref[32:, at])
     twice, less, least = -2.0 * whole, -2.0 * rest, -2.0 * more
     if right_ref is not None:
         write([twice, one, one, one, *norm, one, one, one, *pieces(cross + soft, 3), less, least, twice, twice, less, least, less])
-        right_ref[...] = fact_ref[...].astype(BF16)
+        right_ref[:, at] = fact_ref[:, at].astype(BF16)
     if left_ref is not None:
         write([whole, *norm, one, one, one, *pieces(cross, 3), one, one, one, whole, whole, rest, more, rest, rest, more])
-        for q in range(flat_ref.shape[1] // LANES):
-            at = slice(q * LANES, (q + 1) * LANES)
-            left_ref[at, :] = fact_ref[:, at].T.astype(BF16)
-
-
-def unpack(factor, ref, flat_ref, vec_ref):
+        for q in range(at.start, at.stop, LANES):
+            left_ref[q : q + LANES, :] = fact_ref[:, q : q + LANES].T.astype(BF16)
+
+
+def unpack(factor, ref, span, flat_ref, vec_ref):
     cols = flat_ref.shape[0] - EXTRA
-    for q in range(ref.shape[0]):
+    for q in range(span.start // LANES, span.stop // LANES):
         at = slice(q * LANES, (q + 1) * LANES)
         flat_ref[:, at] = jnp.concatenate([ref[q, n] for n in range(ref.shape[1])], axis=0)
         high, low = split(flat_ref[0:cols, at] * factor)
@@ -183,10 +184,11 @@
 def first_kernel(soft, factor, own_ref, *refs):
     high_ref, low_ref, high_t_ref, low_t_ref, right_ref, acc_ref, flat_ref, vec_ref, left_ref, fact_ref = refs
     panels = vec_ref.shape[1] // PANEL
-    unpack(factor, own_ref, flat_ref, vec_ref)
-    factors(flat_ref, soft, fact_ref, right_ref, left_ref)
     acc_ref[...] = jnp.zeros_like(acc_ref)
     tasks = []
+    whole = slice(0, panels * PANEL)
+    unpack(factor, own_ref, whole, flat_ref, vec_ref)
+    factors(flat_ref, whole, soft, fact_ref, right_ref, left_ref)
     for t, columns, start in near_spans(panels):
         rows = slice(t * PANEL, (t + 1) * PANEL)
         for c in range(columns.start, columns.stop, WIDE):
@@ -204,19 +206,22 @@
                     low_t_ref[to : to + wide - skip, :] = low
                     acc_ref[:, rows] += product(vec_ref[:, at.start + skip : at.stop], high, low)
 
-            tasks.append((rows, at, use))
+            tasks.append((rows, at, use, None))
     evaluate(left_ref, right_ref, tasks, AHEAD)
 
 
 def middle_kernel(soft, factor, own_ref, oth_ref, right_ref, near_ref, *refs):
     high_ref, low_ref, image_ref, flat_ref, vec_ref, left_ref, fact_ref = refs
     cols, half = own_ref.shape[0] - EXTRA, own_ref.shape[1]
-    unpack(factor, oth_ref, flat_ref, vec_ref)
-    factors(flat_ref, soft, fact_ref, None, left_ref)
     image_ref[...] = near_ref[...] + own_ref[0:cols, :] / own_ref[cols + 3 : cols + 4, :]
     tasks = []
     for r in range(0, half, DEEP):
         rows = slice(r, r + DEEP)
+
+        def prepare(rows=rows):
+            unpack(factor, oth_ref, rows, flat_ref, vec_ref)
+            factors(flat_ref, rows, soft, fact_ref, None, left_ref)
+
         for c in range(0, half, BROAD):
             at = slice(c, min(c + BROAD, half))
 
@@ -225,7 +230,7 @@
                 low_ref[rows, at] = low
                 image_ref[:, at] += product(vec_ref[:, rows], high, low)
 
-            tasks.append((rows, at, use))
+            tasks.append((rows, at, use, prepare if c == 0 else None))
     evaluate(left_ref, right_ref, tasks, EARLY)
 
 

time: 47.4 us -> 47.3 us (level)
  no operation moved by 1% of the time
where the time goes in v8:
time: 47.3 us; the launch traced here: 47 us
  blocking collectives  29.4 us (62%)
  Pallas kernels  15.2 us (32%)
  waiting for transfers between devices  1.16 us (2%)
  between operations  0.67 us (1%)
  starting transfers between devices  0.59 us (1%)
    all_to_all x1, blocking collectives, by_columns(): lax.all_to_all(packed, AXES, 0, 0, axis_index_groups=groups, tiled=True)  16 us
    all_to_all x1, blocking collectives, by_columns(): lax.all_to_all(mixed, AXES, 0, 0, axis_index_groups=groups, tiled=True)  13.4 us
    pallas_call x1, Pallas kernels, by_columns(): call(functools.partial(middle_kernel, soft, factor), [shape(half, half, d...  4.38 us
    pallas_call x1, Pallas kernels, by_columns(): call(functools.partial(first_kernel, soft, factor), [shape(PANEL, size, d...  3.88 us
    pallas_call x1, Pallas kernels, by_columns(): call(functools.partial(second_kernel, factor), [shape(cols, half)] * 3 +...  2.57 us
    pallas_call x1, Pallas kernels, by_columns(): call(functools.partial(near_kernel, factor), [shape(cols, half)], [VM] *...  2.42 us
    ppermute x1, waiting for transfers between devices, by_columns(): lax.ppermute(curve, 'col', swap)  1.16 us
    pallas_call x1, Pallas kernels, by_columns(): call(functools.partial(pack_kernel, parts), [shape(parts, cols // EXTRA +...  0.96 us
  transfers between devices with their start and end apart: 3, of which 1 were waited for; matrix products, arithmetic and copies ran while one was open for 0% of the time, Pallas kernels for 13%

profile of v8, /device:TPU:0, one launch (start us, length us, event | category | flops | bytes accessed | tf_op | source)
XLA Modules:
  0.0 47.0 jit_solution(8012159102027096194)
XLA Ops:
  0.6 1.0 %shard_map.50 = f32[16,5,4,128]{3,2,1,0:T(4,128)S(1)} custom-call(f32[3,128]{1,0:T(4,128)} %pos_hbm.1, f32[1,128]{1,0:T(1,128)} %bitcast.1, f32[128,256]{1,0:T(8,128)} %rhs_hbm.1), custom_call_target="tpu_custom_call" | custom-call | tf_op jit(solution)/shard_map/pallas_call | solution.py:343
  1.6 16.0 %all_to_all.10.own_ref = f32[16,5,4,128]{3,2,1,0:T(4,128)S(1)} all-to-all(f32[16,5,4,128]{3,2,1,0:T(4,128)S(1)} %shard_map.50), channel_id=1, replica_groups={{0,2,4,6,8,10,12,14,16,18,20,22,24,26,28,30},{1,3,5,7,9,11,13,15,17,19,..., dimensions={0} | all-to-all | bytes 327680 | tf_op jit(solution)/shard_map/all_to_all | solution.py:354
  17.6 0.0 collective-permute-start
  17.7 3.9 %shard_map.51 = (bf16[256,9216]{1,0:T(8,128)(2,1)S(1)}, bf16[256,9216]{1,0:T(8,128)(2,1)S(1)}, bf16[7168,256]{1,0:T(8,128)(2,1)S(1)}, bf16[7168,256]{1,0:T(8,128...) custom-call(f32[16,5,4,128]{3,2,1,0:T(4,128)S(1)} %all_to_all.10.own_ref), custom_call_target="tpu_custom_call" | custom-call | tf_op jit(solution)/shard_map/pallas_call | solution.py:357
  21.5 0.0 collective-permute-done.oth_ref
  21.5 4.4 %shard_map.52 = (bf16[2048,2048]{1,0:T(8,128)(2,1)S(1)}, bf16[2048,2048]{1,0:T(8,128)(2,1)S(1)}, f32[16,2048]{1,0:T(8,128)S(1)}, f32[20,2048]{1,0:T(8,128)S(1)}) custom-call(f32[20,2048]{1,0:T(8,128)S(1)} %get-tuple-element.18.own_ref, f32[16,5,4,128]{3,2,1,0:T(4,128)S(1)} %collective-permute-done.oth_ref, bf16[48,2048]{1,0:T(8,128)(2,1)S(1)} %get-tuple-element.19.right_ref, ...), custom_call_target="tpu_custom_call" | custom-call | tf_op jit(solution)/shard_map/pallas_call | solution.py:370
  25.9 0.5 %collective-permute-start.1 = (f32[16,2048]{1,0:T(8,128)S(1)}, f32[16,2048]{1,0:T(8,128)S(1)}, u32[]{:S(2)}, u32[]{:S(2)}) collective-permute-start(f32[16,2048]{1,0:T(8,128)S(1)} %get-tuple-element.22.image_ref.im_own_ref), channel_id=1, source_target_pairs={{0,1},{1,0},{2,3},{3,2},{4,5},{5,4},{6,7},{7,6},{8,9},{9,8},{10,11... | collective-permute-start | bytes 393224 | tf_op jit(solution)/shard_map/ppermute | solution.py:381
  26.4 2.4 %shard_map.53.near_ref = f32[16,2048]{1,0:T(8,128)S(1)} custom-call(f32[16,2048]{1,0:T(8,128)S(1)} %get-tuple-element.22.image_ref.im_own_ref, bf16[256,9216]{1,0:T(8,128)(2,1)S(1)} %get-tuple-element.23.high_ref, bf16[256,9216]{1,0:T(8,128)(2,1)S(1)} %get-tuple-element.24.low_ref, bf16[7168,256]{1,0:T(8,128)(2,1)S(1)} %get-tuple-element.25.high_t_ref, ...), custom_call_target="tpu_custom_call" | custom-call | tf_op jit(solution)/shard_map/pallas_call | solution.py:383
  28.8 0.0 collective-permute-done.1.im_oth_ref
  28.8 2.6 %shard_map.54 = (f32[16,2048]{1,0:T(8,128)S(1)}, f32[16,2048]{1,0:T(8,128)S(1)}, f32[16,2048]{1,0:T(8,128)S(1)}, f32[16,128]{1,0:T(8,128)S(1)}, f32[2,16,128]{2,1,0:T(8,128)S(1)}) custom-call(f32[20,2048]{1,0:T(8,128)S(1)} %get-tuple-element.18.own_ref, f32[20,2048]{1,0:T(8,128)S(1)} %get-tuple-element.21.oth_ref, ...), custom_call_target="tpu_custom_call" | custom-call | tf_op jit(solution)/shard_map/pallas_call | solution.py:384
  31.4 0.1 collective-permute-start.2
  31.5 1.2 %collective-permute-done.2.other_ref = f32[16,128]{1,0:T(8,128)S(1)} collective-permute-done((f32[16,128]{1,0:T(8,128)S(1)}, f32[16,128]{1,0:T(8,128)S(1)}, u32[]{:S(2)}, u32[]{:S(2)}) %collective-permute-start.2) | collective-permute-done | bytes 8224 | tf_op jit(solution)/shard_map/ppermute | solution.py:391
  32.7 0.2 shard_map.55
  32.9 13.4 %all_to_all.11.in_ref = f32[16,32,128]{2,1,0:T(8,128)S(1)} all-to-all(f32[16,32,128]{2,1,0:T(8,128)S(1)} %shard_map.55), channel_id=1, replica_groups={{0,2,4,6,8,10,12,14,16,18,20,22,24,26,28,30},{1,3,5,7,9,11,13,15,17,19,..., dimensions={0} | all-to-all | bytes 524288 | tf_op jit(solution)/shard_map/all_to_all | solution.py:393
  46.2 0.8 %shard_map.56 = (f32[128,256]{1,0:T(8,128)}, f32[128,256]{1,0:T(8,128)}) custom-call(f32[16,32,128]{2,1,0:T(8,128)S(1)} %all_to_all.11.in_ref), custom_call_target="tpu_custom_call" | custom-call | tf_op jit(solution)/shard_map/pallas_call | solution.py:395
Async XLA Ops:
  17.6 3.9 %collective-permute-start = (f32[16,5,4,128]{3,2,1,0:T(4,128)S(1)}, f32[16,5,4,128]{3,2,1,0:T(4,128)S(1)}, u32[]{:S(2)}, u32[]{:S(2)}) collective-permute-start(f32[16,5,4,128]{3,2,1,0:T(4,128)S(1)} %all_to_all.10.own_ref), channel_id=1, source_target_pairs={{0,1},{1,0},{2,3},{3,2},{4,5},{5,4},{6,7},{7,6},{8,9},{9,8},{10,11... | collective-permute-start | bytes 491528 | tf_op jit(solution)/shard_map/ppermute | solution.py:355
  25.9 2.9 %collective-permute-start.1 = (f32[16,2048]{1,0:T(8,128)S(1)}, f32[16,2048]{1,0:T(8,128)S(1)}, u32[]{:S(2)}, u32[]{:S(2)}) collective-permute-start(f32[16,2048]{1,0:T(8,128)S(1)} %get-tuple-element.22.image_ref.im_own_ref), channel_id=1, source_target_pairs={{0,1},{1,0},{2,3},{3,2},{4,5},{5,4},{6,7},{7,6},{8,9},{9,8},{10,11... | collective-permute-start | bytes 393224 | tf_op jit(solution)/shard_map/ppermute | solution.py:381
  31.4 1.2 %collective-permute-start.2 = (f32[16,128]{1,0:T(8,128)S(1)}, f32[16,128]{1,0:T(8,128)S(1)}, u32[]{:S(2)}, u32[]{:S(2)}) collective-permute-start(f32[16,128]{1,0:T(8,128)S(1)} %get-tuple-element.32.curve_ref), channel_id=1, source_target_pairs={{0,1},{1,0},{2,3},{3,2},{4,5},{5,4},{6,7},{7,6},{8,9},{9,8},{10,11... | collective-permute-start | bytes 24584 | tf_op jit(solution)/shard_map/ppermute | solution.py:391

commit v9 on v8

--- a/solution.py
+++ b/solution.py
@@ -256,8 +256,8 @@
     for at in places:
         vec_ref[0:cols, at], vec_ref[cols : 2 * cols, at] = split(im_oth_ref[:, at] * factor)
     acc_ref[...] = near_ref[...] + im_own_ref[...] / own_ref[cols + 3 : cols + 4, :]
-    for r in range(0, half, PANEL):
-        rows = slice(r, r + PANEL)
+    for r in range(0, half, 2 * PANEL):
+        rows = slice(r, r + 2 * PANEL)
         acc_ref[...] += product(vec_ref[:, rows], high_ref[rows, :], low_ref[rows, :])
     blocks = [(ref, im, at) for ref, im in ((own_ref, im_own_ref), (oth_ref, im_oth_ref)) for at in places]
     zero = jnp.zeros((cols, LANES), F32)

time: 47.3 us -> 47.3 us (level)
  no operation moved by 1% of the time
where the time goes in v9:
time: 47.3 us; the launch traced here: 47 us
  blocking collectives  29.4 us (62%)
  Pallas kernels  15.2 us (32%)
  waiting for transfers between devices  1.16 us (2%)
  between operations  0.67 us (1%)
  starting transfers between devices  0.59 us (1%)
    all_to_all x1, blocking collectives, by_columns(): lax.all_to_all(packed, AXES, 0, 0, axis_index_groups=groups, tiled=True)  16 us
    all_to_all x1, blocking collectives, by_columns(): lax.all_to_all(mixed, AXES, 0, 0, axis_index_groups=groups, tiled=True)  13.4 us
    pallas_call x1, Pallas kernels, by_columns(): call(functools.partial(middle_kernel, soft, factor), [shape(half, half, d...  4.38 us
    pallas_call x1, Pallas kernels, by_columns(): call(functools.partial(first_kernel, soft, factor), [shape(PANEL, size, d...  3.88 us
    pallas_call x1, Pallas kernels, by_columns(): call(functools.partial(second_kernel, factor), [shape(cols, half)] * 3 +...  2.55 us
    pallas_call x1, Pallas kernels, by_columns(): call(functools.partial(near_kernel, factor), [shape(cols, half)], [VM] *...  2.42 us
    ppermute x1, waiting for transfers between devices, by_columns(): lax.ppermute(curve, 'col', swap)  1.16 us
    pallas_call x1, Pallas kernels, by_columns(): call(functools.partial(pack_kernel, parts), [shape(parts, cols // EXTRA +...  0.96 us
  transfers between devices with their start and end apart: 3, of which 1 were waited for; matrix products, arithmetic and copies ran while one was open for 0% of the time, Pallas kernels for 13%

profile of v9, /device:TPU:0, one launch (start us, length us, event | category | flops | bytes accessed | tf_op | source)
XLA Modules:
  0.0 47.0 jit_solution(468061641108566094)
XLA Ops:
  0.6 1.0 %shard_map.50 = f32[16,5,4,128]{3,2,1,0:T(4,128)S(1)} custom-call(f32[3,128]{1,0:T(4,128)} %pos_hbm.1, f32[1,128]{1,0:T(1,128)} %bitcast.1, f32[128,256]{1,0:T(8,128)} %rhs_hbm.1), custom_call_target="tpu_custom_call" | custom-call | tf_op jit(solution)/shard_map/pallas_call | solution.py:343
  1.6 16.0 %all_to_all.10.own_ref = f32[16,5,4,128]{3,2,1,0:T(4,128)S(1)} all-to-all(f32[16,5,4,128]{3,2,1,0:T(4,128)S(1)} %shard_map.50), channel_id=1, replica_groups={{0,2,4,6,8,10,12,14,16,18,20,22,24,26,28,30},{1,3,5,7,9,11,13,15,17,19,..., dimensions={0} | all-to-all | bytes 327680 | tf_op jit(solution)/shard_map/all_to_all | solution.py:354
  17.6 0.0 collective-permute-start
  17.7 3.9 %shard_map.51 = (bf16[256,9216]{1,0:T(8,128)(2,1)S(1)}, bf16[256,9216]{1,0:T(8,128)(2,1)S(1)}, bf16[7168,256]{1,0:T(8,128)(2,1)S(1)}, bf16[7168,256]{1,0:T(8,128...) custom-call(f32[16,5,4,128]{3,2,1,0:T(4,128)S(1)} %all_to_all.10.own_ref), custom_call_target="tpu_custom_call" | custom-call | tf_op jit(solution)/shard_map/pallas_call | solution.py:357
  21.5 0.0 collective-permute-done.oth_ref
  21.5 4.4 %shard_map.52 = (bf16[2048,2048]{1,0:T(8,128)(2,1)S(1)}, bf16[2048,2048]{1,0:T(8,128)(2,1)S(1)}, f32[16,2048]{1,0:T(8,128)S(1)}, f32[20,2048]{1,0:T(8,128)S(1)}) custom-call(f32[20,2048]{1,0:T(8,128)S(1)} %get-tuple-element.18.own_ref, f32[16,5,4,128]{3,2,1,0:T(4,128)S(1)} %collective-permute-done.oth_ref, bf16[48,2048]{1,0:T(8,128)(2,1)S(1)} %get-tuple-element.19.right_ref, ...), custom_call_target="tpu_custom_call" | custom-call | tf_op jit(solution)/shard_map/pallas_call | solution.py:370
  25.9 0.5 %collective-permute-start.1 = (f32[16,2048]{1,0:T(8,128)S(1)}, f32[16,2048]{1,0:T(8,128)S(1)}, u32[]{:S(2)}, u32[]{:S(2)}) collective-permute-start(f32[16,2048]{1,0:T(8,128)S(1)} %get-tuple-element.22.image_ref.im_own_ref), channel_id=1, source_target_pairs={{0,1},{1,0},{2,3},{3,2},{4,5},{5,4},{6,7},{7,6},{8,9},{9,8},{10,11... | collective-permute-start | bytes 393224 | tf_op jit(solution)/shard_map/ppermute | solution.py:381
  26.4 2.4 %shard_map.53.near_ref = f32[16,2048]{1,0:T(8,128)S(1)} custom-call(f32[16,2048]{1,0:T(8,128)S(1)} %get-tuple-element.22.image_ref.im_own_ref, bf16[256,9216]{1,0:T(8,128)(2,1)S(1)} %get-tuple-element.23.high_ref, bf16[256,9216]{1,0:T(8,128)(2,1)S(1)} %get-tuple-element.24.low_ref, bf16[7168,256]{1,0:T(8,128)(2,1)S(1)} %get-tuple-element.25.high_t_ref, ...), custom_call_target="tpu_custom_call" | custom-call | tf_op jit(solution)/shard_map/pallas_call | solution.py:383
  28.8 0.0 collective-permute-done.1.im_oth_ref
  28.8 2.5 %shard_map.54 = (f32[16,2048]{1,0:T(8,128)S(1)}, f32[16,2048]{1,0:T(8,128)S(1)}, f32[16,2048]{1,0:T(8,128)S(1)}, f32[16,128]{1,0:T(8,128)S(1)}, f32[2,16,128]{2,1,0:T(8,128)S(1)}) custom-call(f32[20,2048]{1,0:T(8,128)S(1)} %get-tuple-element.18.own_ref, f32[20,2048]{1,0:T(8,128)S(1)} %get-tuple-element.21.oth_ref, ...), custom_call_target="tpu_custom_call" | custom-call | tf_op jit(solution)/shard_map/pallas_call | solution.py:384
  31.4 0.1 collective-permute-start.2
  31.5 1.2 %collective-permute-done.2.other_ref = f32[16,128]{1,0:T(8,128)S(1)} collective-permute-done((f32[16,128]{1,0:T(8,128)S(1)}, f32[16,128]{1,0:T(8,128)S(1)}, u32[]{:S(2)}, u32[]{:S(2)}) %collective-permute-start.2) | collective-permute-done | bytes 8224 | tf_op jit(solution)/shard_map/ppermute | solution.py:391
  32.6 0.2 shard_map.55
  32.8 13.4 %all_to_all.11.in_ref = f32[16,32,128]{2,1,0:T(8,128)S(1)} all-to-all(f32[16,32,128]{2,1,0:T(8,128)S(1)} %shard_map.55), channel_id=1, replica_groups={{0,2,4,6,8,10,12,14,16,18,20,22,24,26,28,30},{1,3,5,7,9,11,13,15,17,19,..., dimensions={0} | all-to-all | bytes 524288 | tf_op jit(solution)/shard_map/all_to_all | solution.py:393
  46.2 0.8 %shard_map.56 = (f32[128,256]{1,0:T(8,128)}, f32[128,256]{1,0:T(8,128)}) custom-call(f32[16,32,128]{2,1,0:T(8,128)S(1)} %all_to_all.11.in_ref), custom_call_target="tpu_custom_call" | custom-call | tf_op jit(solution)/shard_map/pallas_call | solution.py:395
Async XLA Ops:
  17.6 3.9 %collective-permute-start = (f32[16,5,4,128]{3,2,1,0:T(4,128)S(1)}, f32[16,5,4,128]{3,2,1,0:T(4,128)S(1)}, u32[]{:S(2)}, u32[]{:S(2)}) collective-permute-start(f32[16,5,4,128]{3,2,1,0:T(4,128)S(1)} %all_to_all.10.own_ref), channel_id=1, source_target_pairs={{0,1},{1,0},{2,3},{3,2},{4,5},{5,4},{6,7},{7,6},{8,9},{9,8},{10,11... | collective-permute-start | bytes 491528 | tf_op jit(solution)/shard_map/ppermute | solution.py:355
  25.9 2.9 %collective-permute-start.1 = (f32[16,2048]{1,0:T(8,128)S(1)}, f32[16,2048]{1,0:T(8,128)S(1)}, u32[]{:S(2)}, u32[]{:S(2)}) collective-permute-start(f32[16,2048]{1,0:T(8,128)S(1)} %get-tuple-element.22.image_ref.im_own_ref), channel_id=1, source_target_pairs={{0,1},{1,0},{2,3},{3,2},{4,5},{5,4},{6,7},{7,6},{8,9},{9,8},{10,11... | collective-permute-start | bytes 393224 | tf_op jit(solution)/shard_map/ppermute | solution.py:381
  31.4 1.2 %collective-permute-start.2 = (f32[16,128]{1,0:T(8,128)S(1)}, f32[16,128]{1,0:T(8,128)S(1)}, u32[]{:S(2)}, u32[]{:S(2)}) collective-permute-start(f32[16,128]{1,0:T(8,128)S(1)} %get-tuple-element.32.curve_ref), channel_id=1, source_target_pairs={{0,1},{1,0},{2,3},{3,2},{4,5},{5,4},{6,7},{7,6},{8,9},{9,8},{10,11... | collective-permute-start | bytes 24584 | tf_op jit(solution)/shard_map/ppermute | solution.py:391
